TPU v7x, 256 devices: a whole 4x4x8 slice. The times are simulated.
256 devices in a mesh: dp: 16 (over y, z_hi, core), mx: 4 (over z_lo), my: 4 (over x).
Axes of the slice: x: 4, y: 4, z: 8 (z_hi: 2, z_lo: 4; z = z_hi * 4 + z_lo), core: 2. Of those that a mesh axis runs over, the one named last changes fastest.
Arguments:
- features: bfloat16 [128, 128, 3072], P('dp', None, 'mx'), may hold values from -6 to 6
- segment_ids: int32 [128, 128], P('dp'), may hold values from 0 to 3, never falling along the last dimension, each value on 1 to 80 neighbouring positions
- owners: int32 [16, 8], replicated, may hold values from 0 to 15, as said below
- w_qkv: bfloat16 [3072, 9216], P('mx', 'my'), may hold values from -0.109375 to 0.109375
- w_out: bfloat16 [3072, 3072], P('my', 'mx'), may hold values from -0.109375 to 0.109375
- cotangent: bfloat16 [128, 128, 3072], P('dp', None, 'mx'), may hold values from -6 to 6
Outputs:
- grad_features: bfloat16 [128, 128, 3072], P('dp', 'my', 'mx')
- grad_qkv: float32 [4, 768, 9216], P('mx', 'dp', 'my')
- grad_out: float32 [4, 768, 3072], P('my', 'dp', 'mx')
Inputs may be any that keep to these rules, and one draw needn't show every extreme that they name: For each tile position the 16 loaders send to 16 different owners, so every owner receives exactly 8 tiles; one loader sends at most 1 tiles to one owner, and some loader sends exactly 1. `segment_ids`: within a tile the ids never fall; an image covers 1 to 80 patches.
All inputs are finite; a program needn't handle non-finite values.
Results may differ from a plain program's by a relative error of at most 0.035.
Values may be sent and summed in bfloat16 or wider, within the bound.
A program may use at most 64 MiB of HBM per device.

v0:
```python
import jax
import jax.numpy as jnp
from jax import lax
from jax.sharding import PartitionSpec as P

HEAD = 128


def product(pattern, operand_a, operand_b):
    return jnp.einsum(pattern, operand_a, operand_b, preferred_element_type=jnp.float32)


def normalize(values):
    centered = values - jnp.mean(values, axis=-1, keepdims=True)
    inverse = lax.rsqrt(jnp.mean(centered * centered, axis=-1, keepdims=True) + 1e-06)
    return (centered * inverse, inverse)


def norm_back(grad_hat, normed, inverse):
    return inverse * (
        grad_hat
        - jnp.mean(grad_hat, axis=-1, keepdims=True)
        - normed * jnp.mean(grad_hat * normed, axis=-1, keepdims=True)
    )


def attend_both(qkv_rows, grad_rows, image_ids):
    length, breadth = qkv_rows.shape
    heads_here = breadth // (3 * HEAD)
    pieces = qkv_rows.reshape(length, heads_here, 3, HEAD)
    query_hat, query_inv = normalize(pieces[:, :, 0])
    key_hat, key_inv = normalize(pieces[:, :, 1])
    query_bf = query_hat.astype(jnp.bfloat16)
    key_bf = key_hat.astype(jnp.bfloat16)
    value_bf = pieces[:, :, 2].astype(jnp.bfloat16)
    score_scale = HEAD ** (-0.5)
    scores = product("qhe,khe->hqk", query_bf, key_bf) * score_scale
    same_image = image_ids[:, None] == image_ids[None, :]
    expo = jnp.where(same_image[None], jnp.exp(scores), 0.0)
    weights = expo / jnp.sum(expo, axis=-1, keepdims=True)
    weights_bf = weights.astype(jnp.bfloat16)
    attended = product("hqk,khe->qhe", weights_bf, value_bf)
    grad_bf = grad_rows.reshape(length, heads_here, HEAD).astype(jnp.bfloat16)
    grad_value = product("hqk,qhe->khe", weights_bf, grad_bf)
    grad_weights = product("qhe,khe->hqk", grad_bf, value_bf)
    grad_scores = (
        weights
        * (grad_weights - jnp.sum(weights * grad_weights, axis=-1, keepdims=True))
        * score_scale
    )
    grad_scores_bf = grad_scores.astype(jnp.bfloat16)
    grad_query = norm_back(product("hqk,khe->qhe", grad_scores_bf, key_bf), query_hat, query_inv)
    grad_key = norm_back(product("hqk,qhe->khe", grad_scores_bf, query_bf), key_hat, key_inv)
    grad_qkv = (
        jnp.stack([grad_query, grad_key, grad_value], axis=2)
        .reshape(length, breadth)
        .astype(jnp.bfloat16)
    )
    return (attended.reshape(length, heads_here * HEAD).astype(jnp.bfloat16), grad_qkv)


def shards(features, segment_ids, owners, w_qkv, w_out, cotangent):
    group_count = lax.axis_size("dp")
    tile_count, patch_count, feature_width = features.shape
    capacity = (tile_count + group_count - 1) // group_count
    slot_total = group_count * capacity
    loader_index = lax.axis_index("dp")
    own_row = lax.dynamic_slice_in_dim(owners, loader_index, 1, 0)[0]
    positions = jnp.arange(tile_count)
    same_owner = own_row[:, None] == own_row[None, :]
    slot_rank = jnp.sum(same_owner & (positions[None, :] < positions[:, None]), axis=1)
    slot_index = jnp.arange(slot_total)
    matches = (own_row[None, :] == (slot_index // capacity)[:, None]) & (
        slot_rank[None, :] == (slot_index % capacity)[:, None]
    )
    chosen = jnp.sum(jnp.where(matches, positions[None, :], 0), axis=1)
    filled = jnp.any(matches, axis=1)
    send_rows = jnp.where(
        filled[:, None, None], jnp.take(features, chosen, axis=0), jnp.zeros((), jnp.bfloat16)
    )
    send_ids = jnp.where(filled[:, None], jnp.take(segment_ids, chosen, axis=0), 0).astype(
        jnp.bfloat16
    )
    got_rows, got_ids = (
        lax.all_to_all(send_rows, "dp", split_axis=0, concat_axis=0, tiled=True),
        lax.all_to_all(send_ids, "dp", split_axis=0, concat_axis=0, tiled=True),
    )
    arrivals = jnp.sum(owners == loader_index, axis=1)
    live_slot = slot_index % capacity < jnp.repeat(arrivals, capacity)
    live_rank = jnp.cumsum(live_slot.astype(jnp.int32)) - 1
    picked = jnp.sum(
        jnp.where(
            live_slot[None, :] & (live_rank[None, :] == positions[:, None]), slot_index[None, :], 0
        ),
        axis=1,
    )
    owned_rows = jnp.take(got_rows, picked, axis=0)
    owned_ids = jnp.take(got_ids, picked, axis=0).astype(jnp.int32)
    row_total = tile_count * patch_count
    flat_rows = owned_rows.reshape(row_total, feature_width)
    flat_grad = cotangent.reshape(row_total, feature_width)
    qkv_width = w_qkv.shape[1]
    out_width = w_out.shape[0]
    model_count = lax.axis_size("mx")
    rows_here = flat_rows
    grad_here = flat_grad
    projected = jnp.dot(rows_here, w_qkv, preferred_element_type=jnp.float32)
    returned = lax.dot_general(
        grad_here, w_out, (((1,), (1,)), ((), ())), preferred_element_type=jnp.float32
    )
    shares = lax.psum_scatter(
        jnp.concatenate([projected, returned], axis=1).astype(jnp.bfloat16),
        "mx",
        scatter_dimension=0,
        tiled=True,
    ).astype(jnp.float32)
    my_tiles = tile_count // model_count
    shares = shares.reshape(my_tiles, patch_count, qkv_width + out_width)
    tile_ids = lax.dynamic_slice_in_dim(owned_ids, lax.axis_index("mx") * my_tiles, my_tiles, 0)
    attended, grad_qkv = jax.vmap(attend_both)(
        shares[:, :, :qkv_width], shares[:, :, qkv_width:], tile_ids
    )
    local_rows = jnp.concatenate([attended, grad_qkv], axis=2).reshape(
        my_tiles * patch_count, out_width + qkv_width
    )
    shard_rows = lax.all_gather(local_rows, "mx", axis=0, tiled=True)
    rows_here = flat_rows
    grad_here = flat_grad
    attended_part = shard_rows[:, :out_width]
    grad_part = shard_rows[:, out_width:]
    new_qkv = lax.dot_general(
        rows_here, grad_part, (((0,), (0,)), ((), ())), preferred_element_type=jnp.float32
    )
    new_out = lax.dot_general(
        attended_part, grad_here, (((0,), (0,)), ((), ())), preferred_element_type=jnp.float32
    )
    back_rows = lax.dot_general(
        grad_part, w_qkv, (((1,), (1,)), ((), ())), preferred_element_type=jnp.float32
    )
    grad_features = lax.psum_scatter(
        back_rows.reshape(tile_count, patch_count, feature_width).astype(jnp.bfloat16),
        "my",
        scatter_dimension=1,
        tiled=True,
    )
    summed_qkv, summed_out = (
        lax.psum_scatter(
            new_qkv[None].astype(jnp.bfloat16), "dp", scatter_dimension=1, tiled=True
        ).astype(jnp.float32),
        lax.psum_scatter(
            new_out[None].astype(jnp.bfloat16), "dp", scatter_dimension=1, tiled=True
        ).astype(jnp.float32),
    )
    inverse_groups = 1.0 / group_count
    return (grad_features, summed_qkv * inverse_groups, summed_out * inverse_groups)


def solution(mesh):
    return jax.shard_map(
        shards,
        mesh=mesh,
        in_specs=(
            P("dp", None, "mx"),
            P("dp", None),
            P(),
            P("mx", "my"),
            P("my", "mx"),
            P("dp", None, "mx"),
        ),
        out_specs=(P("dp", "my", "mx"), P("mx", "dp", "my"), P("my", "dp", "mx")),
        check_vma=False,
    )
```

profile of v0, /device:TPU:1, one launch (start us, length us, event | category | flops | bytes accessed | tf_op | source)
XLA Modules:
  0.0 607.0 jit_solution(1828036162220122600)
XLA Ops:
  7.2 1.0 dynamic-slice_reduce_fusion
  8.2 0.2 convert_reduce_fusion
  8.4 0.1 select_reduce_fusion
  8.5 0.1 fusion.49
  8.6 3.9 gather_fusion
  12.5 4.0 select_select_fusion
  16.5 12.7 %all-to-all-start = ((bf16[16,128,768]{2,1,0:T(8,128)(2,1)}), bf16[16,128,768]{2,1,0:T(8,128)(2,1)}, u32[]{:S(2)}, u32[]{:S(2)}) async-start(bf16[16,128,768]{2,1,0:T(8,128)(2,1)} %select_select_fusion), calls=%async_computation | async-start | bytes 6291456 | tf_op jit(solution)/shard_map/all_to_all | solution.py:85
  29.3 0.5 broadcast_compare_fusion.2
  29.9 0.1 copy.69
  30.0 0.1 add_reduce_fusion
  30.1 0.8 select_reduce_fusion.1
  31.0 4.3 convolution_convert_fusion.2
  35.3 46.1 %all-to-all-done = bf16[16,128,768]{2,1,0:T(8,128)(2,1)} async-done(((bf16[16,128,768]{2,1,0:T(8,128)(2,1)}), bf16[16,128,768]{2,1,0:T(8,128)(2,1)}, u32[]{:S(2)}, u32[]{:S(2)}) %all-to-all-start) | async-done | bytes 3145760 | tf_op jit(solution)/shard_map/all_to_all | solution.py:85
  81.4 3.7 gather_fusion.1
  85.1 1.6 bitcast_select_fusion
  86.7 1.1 copy-done.5
  87.9 4.0 convolution_convert_fusion
  91.9 3.5 pad_maximum_fusion
  95.5 0.7 copy-done.8
  96.1 0.7 gather_fusion.2
  96.8 0.8 fusion.46
  97.6 0.6 copy.73
  98.2 27.3 %all-to-all-start.1 = ((bf16[16,1,128]{2,1,0:T(2,128)(2,1)}), bf16[16,1,128]{2,1,0:T(2,128)(2,1)S(1)}, u32[]{:S(2)}, u32[]{:S(2)}) async-start(bf16[16,1,128]{2,1,0:T(2,128)(2,1)} %copy.73), calls=%async_computation.2 | async-start | bytes 16384 | tf_op jit(solution)/shard_map/all_to_all | solution.py:86
  125.5 9.3 %all-to-all-done.1 = bf16[16,1,128]{2,1,0:T(2,128)(2,1)S(1)} async-done(((bf16[16,1,128]{2,1,0:T(2,128)(2,1)}), bf16[16,1,128]{2,1,0:T(2,128)(2,1)S(1)}, u32[]{:S(2)}, u32[]{:S(2)}) %all-to-all-start.1) | async-done | bytes 4128 | tf_op jit(solution)/shard_map/all_to_all | solution.py:86
  134.9 0.6 gather_fusion.3
  135.4 0.7 select_convert_fusion
  136.2 0.7 broadcast_compare_fusion
  136.9 94.5 %reduce-scatter.5.cloned.1.call-done = bf16[256,3072]{1,0:T(8,128)(2,1)} async-done(((bf16[1024,3072]{1,0:T(8,128)(2,1)}), bf16[256,3072]{1,0:T(8,128)(2,1)}) %reduce-scatter.5.cloned.1.call-update) | async-done | bytes 1572880 | tf_op jit(solution)/shard_map/reduce_scatter | solution.py:111
  231.4 2.5 slice.39
  233.9 1.8 slice.43
  235.7 2.4 copy.96
  238.0 2.8 fusion.57
  240.8 0.1 slice_reduce_fusion
  240.9 1.3 copy-done.1
  242.2 0.2 multiply_reduce_fusion.3
  242.4 0.6 add_rsqrt_fusion
  243.0 1.9 copy.97
  244.9 2.7 fusion.35
  247.6 1.6 fusion.22
  249.2 2.3 fusion.38
  251.5 1.1 fusion.23
  252.7 0.4 copy.78
  253.1 0.8 copy.106
  253.9 3.4 convolution_bitcast_fusion
  257.3 4.9 multiply_reduce_fusion.2
  262.2 0.7 broadcast_multiply_fusion
  262.9 0.7 broadcast_multiply_fusion.1
  263.6 0.7 broadcast_multiply_fusion.2
  264.3 0.7 broadcast_multiply_fusion.3
  265.0 2.4 fusion.32
  267.4 0.1 pad_maximum_fusion.2
  267.6 1.2 copy.85
  268.8 0.2 copy.105
  269.0 1.2 pad_maximum_fusion.1
  270.2 0.2 reduce-scatter.11.cloned.1.call-start
  270.5 121.2 %all-gather.2.cloned.1.call-done = bf16[1024,3072]{0,1:T(8,128)(2,1)} async-done(((bf16[256,3072]{0,1:T(8,128)(2,1)}), bf16[1024,3072]{0,1:T(8,128)(2,1)}) %all-gather.2.cloned.1.call-update) | async-done | bytes 6291472 | tf_op jit(solution)/shard_map/all_gather | solution.py:126
  391.7 4.3 fusion.13
  396.0 8.5 %fusion.1 = bf16[1,768,2304]{2,1,0:T(8,128)(2,1)} fusion(bf16[1024,768]{1,0:T(8,128)(2,1)} %copy-done.5, bf16[1024,3072]{0,1:T(8,128)(2,1)} %all-gather.2.cloned.1.call-done), kind=kOutput, calls=%fused_computation.8 | convolution fusion | flops 3625648128 | bytes 9830400 | tf_op jit(solution)/shard_map/dot_general | solution.py:131
  404.6 7.4 %fusion.5 = bf16[1024,768]{1,0:T(8,128)(2,1)} fusion(bf16[768,2304]{1,0:T(8,128)(2,1)S(1)} %copy-done, bf16[1024,3072]{0,1:T(8,128)(2,1)} %all-gather.2.cloned.1.call-done), kind=kOutput, calls=%fused_computation.13 | convolution fusion | flops 3624665088 | bytes 9830400 | tf_op jit(solution)/shard_map/dot_general | solution.py:137
  412.0 60.8 %reduce-scatter.11.cloned.1.call-done = bf16[1,48,768]{2,1,0:T(8,128)(2,1)} async-done(((bf16[1,768,768]{2,1,0:T(8,128)(2,1)}), bf16[1,48,768]{2,1,0:T(8,128)(2,1)}) %reduce-scatter.11.cloned.1.call-update) | async-done | bytes 73744 | tf_op jit(solution)/shard_map/reduce_scatter | solution.py:150
  472.8 1.6 convert_multiply_fusion.1
  474.4 98.5 %reduce-scatter.9.cloned.1.call-done = bf16[1,48,2304]{2,1,0:T(8,128)(2,1)} async-done(((bf16[1,768,2304]{2,1,0:T(8,128)(2,1)}), bf16[1,48,2304]{2,1,0:T(8,128)(2,1)}) %reduce-scatter.9.cloned.1.call-update) | async-done | bytes 221200 | tf_op jit(solution)/shard_map/reduce_scatter | solution.py:147
  572.9 1.7 convert_multiply_fusion
  574.6 25.9 %reduce-scatter.7.cloned.1.call-done = bf16[8,32,768]{2,1,0:T(8,128)(2,1)} async-done(((bf16[8,128,768]{2,1,0:T(8,128)(2,1)}), bf16[8,32,768]{2,1,0:T(8,128)(2,1)}) %reduce-scatter.7.cloned.1.call-update) | async-done | bytes 393232 | tf_op jit(solution)/shard_map/reduce_scatter | solution.py:140
  (50 shorter events, 0.5 us)
Async XLA Ops:
  7.2 80.7 %copy-start = (bf16[768,2304]{1,0:T(8,128)(2,1)S(1)}, bf16[768,2304]{1,0:T(8,128)(2,1)}, u32[]{:S(2)}) copy-start(bf16[768,2304]{1,0:T(8,128)(2,1)} %param.9) | copy-start | bytes 10616836
  8.5 4.0 copy-start.12
  8.6 3.9 copy-start.13
  8.6 3.9 copy-start.11
  16.5 12.8 %copy-start.10 = (s32[16,8]{0,1:T(8,128)S(1)}, s32[16,8]{0,1:T(8,128)}, u32[]{:S(2)}) copy-start(s32[16,8]{0,1:T(8,128)} %param.8) | copy-start | bytes 1540
  16.5 64.9 %all-to-all-start = ((bf16[16,128,768]{2,1,0:T(8,128)(2,1)}), bf16[16,128,768]{2,1,0:T(8,128)(2,1)}, u32[]{:S(2)}, u32[]{:S(2)}) async-start(bf16[16,128,768]{2,1,0:T(8,128)(2,1)} %select_select_fusion), calls=%async_computation | async-start | bytes 6291456 | tf_op jit(solution)/shard_map/all_to_all | solution.py:85
  29.3 202.2 %reduce-scatter.5.cloned.1.call-start = ((), (), s32[]{:S(2)}) async-start(), calls=%async_computation.6 | async-start | bytes 7864320 | tf_op jit(solution)/shard_map/reduce_scatter | solution.py:111
  30.9 4.4 copy-start.14
  86.7 1.1 copy-start.5
  87.9 4.1 copy-start.4
  95.5 0.7 copy-start.8
  98.2 36.7 %all-to-all-start.1 = ((bf16[16,1,128]{2,1,0:T(2,128)(2,1)}), bf16[16,1,128]{2,1,0:T(2,128)(2,1)S(1)}, u32[]{:S(2)}, u32[]{:S(2)}) async-start(bf16[16,1,128]{2,1,0:T(2,128)(2,1)} %copy.73), calls=%async_computation.2 | async-start | bytes 16384 | tf_op jit(solution)/shard_map/all_to_all | solution.py:86
  125.5 266.2 %all-gather.2.cloned.1.call-start = ((), (), s32[]{:S(2)}) async-start(), calls=%async_computation.7 | async-start | bytes 7864320 | tf_op jit(solution)/shard_map/all_gather | solution.py:126
  240.8 1.4 copy-start.1
  240.9 2.1 copy-start.9
  247.6 3.9 copy-start.2
  247.6 3.9 copy-start.3
  262.2 5.2 copy-start.7
  267.6 1.4 copy-start.6
  270.2 202.6 %reduce-scatter.11.cloned.1.call-start = ((), (), s32[]{:S(2)}) async-start(), calls=%async_computation.10 | async-start | bytes 1253376 | tf_op jit(solution)/shard_map/reduce_scatter | solution.py:150
  396.0 176.9 %reduce-scatter.9.cloned.1.call-start = ((), (), s32[]{:S(2)}) async-start(), calls=%async_computation.9 | async-start | bytes 3760128 | tf_op jit(solution)/shard_map/reduce_scatter | solution.py:147
  404.6 196.0 %reduce-scatter.7.cloned.1.call-start = ((), (), s32[]{:S(2)}) async-start(), calls=%async_computation.8 | async-start | bytes 1966080 | tf_op jit(solution)/shard_map/reduce_scatter | solution.py:140
Sparse Core Ops, SparseCore 0:
  95.6 135.7 reduce-scatter.4
  270.4 121.2 all-gather.1
  396.1 76.6 reduce-scatter.10
  477.7 95.2 reduce-scatter.8
  576.1 24.4 reduce-scatter.6
where the time goes:
time: 608 us; the launch traced here: 607 us
  waiting for transfers between devices  456 us (75%)
  matrix products  44.6 us (7%)
  starting transfers between devices  40.4 us (7%)
  other arithmetic  26.8 us (4%)
  local copies, waits for them, and re-layouts  24.8 us (4%)
  between operations  14 us (2%)
    all_gather x1, waiting for transfers between devices, shards(): shard_rows = lax.all_gather(local_rows, 'mx', axis=0, tiled=True)  121 us
    reduce_scatter x1, waiting for transfers between devices, shards(): lax.psum_scatter(new_qkv[None].astype(jnp.bfloat16), 'dp', scatter_dimens...  98.5 us
    reduce_scatter x1, waiting for transfers between devices, shards(): lax.psum_scatter(jnp.concatenate([projected, returned], axis=1).astype(jn...  94.5 us
    reduce_scatter x1, waiting for transfers between devices, shards(): lax.psum_scatter(new_out[None].astype(jnp.bfloat16), 'dp', scatter_dimens...  60.8 us
    all_to_all x1, waiting for transfers between devices, shards(): lax.all_to_all(send_rows, 'dp', split_axis=0, concat_axis=0, tiled=True)  46.1 us
    all_to_all x1, starting transfers between devices, shards(): lax.all_to_all(send_ids, 'dp', split_axis=0, concat_axis=0, tiled=True)  27.3 us
    reduce_scatter x1, waiting for transfers between devices, shards(): lax.psum_scatter(back_rows.reshape(tile_count, patch_count, feature_width...  25.9 us
    dot_general x5, matrix products, product(): jnp.einsum(pattern, operand_a, operand_b, preferred_element_type=jnp.floa...  13.4 us
  transfers between devices with their start and end apart: 7, of which 7 were waited for; matrix products, arithmetic and copies ran while one was open for 5% of the time, Pallas kernels for 0%

commit v1 on v0

v1 whole, which is shorter than its diff:
```python
import jax
import jax.numpy as jnp
from jax import lax
from jax.experimental import pallas as pl
from jax.experimental.pallas import tpu as pltpu
from jax.sharding import PartitionSpec as P

HEAD = 128
HEADS_HERE = 6
TILES = 8
HALF = 4
UNITS = HEADS_HERE * HALF
PATCH = 128
WIDE = 768
QKV = 3 * HEAD
UNIT = QKV + HEAD
CHUNKS = 8
BF = jnp.bfloat16
F32 = jnp.float32
MESH = pl.DeviceIdType.MESH
SCALE = HEAD ** (-0.5)


def dot(a, b, contract):
    return lax.dot_general(a, b, ((contract[0], contract[1]), ((), ())), preferred_element_type=F32)


NN = ((1,), (0,))
NT = ((1,), (1,))
TN = ((0,), (0,))


def normalize(values):
    centered = values - jnp.mean(values, axis=-1, keepdims=True)
    inverse = lax.rsqrt(jnp.mean(centered * centered, axis=-1, keepdims=True) + 1e-06)
    return centered * inverse, inverse


def norm_back(grad_hat, normed, inverse):
    return inverse * (
        grad_hat
        - jnp.mean(grad_hat, axis=-1, keepdims=True)
        - normed * jnp.mean(grad_hat * normed, axis=-1, keepdims=True)
    )


def attend(total, mask):
    query_hat, query_inv = normalize(total[:, :HEAD])
    key_hat, key_inv = normalize(total[:, HEAD : 2 * HEAD])
    query_bf = query_hat.astype(BF)
    key_bf = key_hat.astype(BF)
    value_bf = total[:, 2 * HEAD : 3 * HEAD].astype(BF)
    grad_bf = total[:, 3 * HEAD :].astype(BF)
    expo = jnp.exp(dot(query_bf, key_bf, NT) * SCALE) * mask
    weights = expo / jnp.sum(expo, axis=-1, keepdims=True)
    weights_bf = weights.astype(BF)
    attended = dot(weights_bf, value_bf, NN)
    grad_value = dot(weights_bf, grad_bf, TN)
    grad_weights = dot(grad_bf, value_bf, NT)
    grad_scores = (
        weights
        * (grad_weights - jnp.sum(weights * grad_weights, axis=-1, keepdims=True))
        * SCALE
    ).astype(BF)
    grad_query = norm_back(dot(grad_scores, key_bf, NN), query_hat, query_inv)
    grad_key = norm_back(dot(grad_scores, query_bf, TN), key_hat, key_inv)
    return jnp.concatenate([attended, grad_query, grad_key, grad_value], axis=1).astype(BF)


def branch(
    quarter, cot, w_qkv, w_out, mask,
    out_feat, out_qkv, out_out,
    feat, feat_t, part, chain, found, grads, core_in, core_sum, y_in, y_sum, z_in,
    grad_wide, feat_acc, feat_bf, feat_in,
    x_send, x_recv, b_send, b_recv, c_send, c_recv,
    core_send, core_recv, y_send, y_recv, z_send, z_recv, d_send, d_recv,
):
    dp = lax.axis_index("dp")
    mx = lax.axis_index("mx")
    my = lax.axis_index("my")
    core = lax.rem(dp, 2)
    high = lax.rem(dp // 2, 2)
    row = dp // 4
    is_end = (mx == 0) | (mx == 3)
    is_mid = (mx == 1) | (mx == 2)
    own = jnp.where(mx == 0, 0, HALF)
    other = HALF - own
    near = jnp.where(mx == 0, 1, 2)

    core_peer = (dp + 1 - 2 * core, mx, my)
    high_peer = (row * 4 + (1 - high) * 2 + core, mx, my)

    def row_peer(step):
        return (lax.rem(row + step, 4) * 4 + lax.rem(dp, 4), mx, my)

    def x_peer(step):
        return (dp, mx, lax.rem(my + step, 4))

    def along(to):
        return (dp, to, my)

    barrier = pltpu.get_barrier_semaphore()

    def greet(peer):
        pl.semaphore_signal(barrier, inc=1, device_id=peer, device_id_type=MESH)

    greet(core_peer)
    greet(high_peer)
    for step in range(1, 4):
        greet(row_peer(step))
        greet(x_peer(step))

    @pl.when(is_end)
    def _():
        greet(along(near))
        pl.semaphore_wait(barrier, 9)

    @pl.when(is_mid)
    def _():
        greet(along(mx - 1))
        greet(along(mx + 1))
        pl.semaphore_wait(barrier, 10)

    def remote(src, dst, send, recv, peer):
        return pltpu.make_async_remote_copy(
            src_ref=src, dst_ref=dst, send_sem=send, recv_sem=recv,
            device_id=peer, device_id_type=MESH,
        )

    mine = pl.ds(pl.multiple_of(my * 32, 32), 32)

    def x_copy(step):
        return remote(
            quarter, feat.at[:, mine], x_send.at[step - 1], x_recv.at[step - 1], x_peer(step)
        )

    for step in (2, 1, 3):
        x_copy(step).start()
    feat[:, mine, :] = quarter[...]
    for step in (1, 3, 2):
        x_copy(step).wait_recv()
    for step in range(1, 4):
        x_copy(step).wait_send()

    def project(unit):
        head = unit // HALF
        tile = lax.rem(unit, HALF)
        rows = jnp.concatenate([feat[tile], feat[tile + HALF]], axis=0)
        columns = pl.ds(pl.multiple_of(head * QKV, HEAD), QKV)
        product = dot(rows, w_qkv[:, columns], NN).astype(BF)
        rows = jnp.concatenate([cot[tile], cot[tile + HALF]], axis=0)
        lines = pl.ds(pl.multiple_of(head * HEAD, HEAD), HEAD)
        back = dot(rows, w_out[lines, :], NT).astype(BF)
        part[head, tile, :, :QKV] = product[:PATCH]
        part[head, tile + HALF, :, :QKV] = product[PATCH:]
        part[head, tile, :, QKV:] = back[:PATCH]
        part[head, tile + HALF, :, QKV:] = back[PATCH:]

    def b_copy(head, tile, to):
        return remote(
            part.at[head, tile], chain.at[head, tile], b_send, b_recv.at[head, tile], along(to)
        )

    def c_copy(head, tile, to):
        return remote(
            found.at[head, tile], found.at[head, tile], c_send, c_recv.at[head, tile], along(to)
        )

    @pl.when(is_end)
    def _():
        def send_out(unit, carry):
            project(unit)
            b_copy(unit // HALF, other + lax.rem(unit, HALF), near).start()
            return carry

        lax.fori_loop(0, UNITS, send_out, 0)

        def finish(unit, carry):
            head = unit // HALF
            tile = own + lax.rem(unit, HALF)
            b_copy(head, tile, near).wait_recv()
            total = part[head, tile].astype(F32) + chain[head, tile].astype(F32)
            found[head, tile] = attend(total, mask[tile])
            c_copy(head, tile, near).start()
            return carry

        lax.fori_loop(0, UNITS, finish, 0)

    @pl.when(is_mid)
    def _():
        def prepare(unit, carry):
            project(unit)
            return carry

        lax.fori_loop(0, HALF, prepare, 0)

        def pass_on(unit, carry):
            head = unit // HALF
            at = lax.rem(unit, HALF)
            for tile, to in ((at + HALF, mx + 1), (at, mx - 1)):
                b_copy(head, tile, to).wait_recv()
                part[head, tile] = (
                    part[head, tile].astype(F32) + chain[head, tile].astype(F32)
                ).astype(BF)
                b_copy(head, tile, to).start()

            @pl.when(unit + HALF < UNITS)
            def _():
                project(unit + HALF)

            return carry

        lax.fori_loop(0, UNITS, pass_on, 0)

    feat_acc[...] = jnp.zeros_like(feat_acc)

    def core_copy(chunk):
        return remote(
            grads.at[chunk, :, 1 - core], core_in.at[chunk],
            core_send.at[chunk], core_recv.at[chunk], core_peer,
        )

    def y_copy(chunk, step):
        return remote(
            core_sum.at[chunk, pl.ds(2 * lax.rem(row + step, 4), 2)], y_in.at[chunk, step - 1],
            y_send.at[chunk, step - 1], y_recv.at[chunk, step - 1], row_peer(step),
        )

    def z_copy(chunk):
        return remote(
            y_sum.at[chunk, 1 - high], z_in.at[chunk],
            z_send.at[chunk], z_recv.at[chunk], high_peer,
        )

    def stage_core(chunk):
        core_copy(chunk).wait_recv()
        core_sum[chunk] = (
            grads[chunk, :, core].astype(F32) + core_in[chunk].astype(F32)
        ).astype(BF)
        for step in (2, 1, 3):
            y_copy(chunk, step).start()

    def stage_row(chunk):
        total = core_sum[chunk, pl.ds(2 * row, 2)].astype(F32)
        for step in (1, 3, 2):
            y_copy(chunk, step).wait_recv()
            total = total + y_in[chunk, step - 1].astype(F32)
        y_sum[chunk] = total.astype(BF)
        z_copy(chunk).start()

    def stage_high(chunk):
        z_copy(chunk).wait_recv()
        return (y_sum[chunk, high].astype(F32) + z_in[chunk].astype(F32)) * (1.0 / 16.0)

    def store_qkv(chunk):
        columns = pl.ds(pl.multiple_of(chunk * QKV, HEAD), QKV)
        out_qkv[0, :, columns] = stage_high(chunk)

    def weight_step(unit, carry):
        at = lax.rem(unit, HALF)

        @pl.when(unit < UNITS)
        def _():
            head = unit // HALF

            @pl.when(is_mid)
            def _():
                for tile, to in ((at, mx + 1), (at + HALF, mx - 1)):
                    c_copy(head, tile, to).wait_recv()
                    c_copy(head, tile, to).start()

            @pl.when(is_end)
            def _():
                c_copy(head, other + at, near).wait_recv()

        @pl.when(unit < HALF)
        def _():
            for tile in range(2):
                columns = pl.ds(pl.multiple_of((2 * at + tile) * PATCH, PATCH), PATCH)
                feat_t[:, columns] = feat[2 * at + tile].T

        @pl.when(unit >= HALF)
        def _():
            head = unit // HALF - 1
            grad = found[head, :, :, HEAD:].reshape(TILES * PATCH, QKV)
            lines = pl.ds(pl.multiple_of(at * 192, 64), 192)
            piece = dot(feat_t[lines, :], grad, NN).astype(BF)
            grads[head, pl.ds(2 * at, 2)] = piece.reshape(2, 2, 48, QKV)
            tiles = pl.ds(2 * at, 2)
            columns = pl.ds(pl.multiple_of(head * QKV, HEAD), QKV)
            back = dot(
                found[head, tiles, :, HEAD:].reshape(2 * PATCH, QKV), w_qkv[:, columns], NT
            )
            feat_acc[tiles] += back.reshape(2, PATCH, WIDE)

            @pl.when(at == 0)
            def _():
                lines = pl.ds(pl.multiple_of(head * HEAD, HEAD), HEAD)
                grad_wide[lines, :] = dot(
                    found[head, :, :, :HEAD].reshape(TILES * PATCH, HEAD),
                    cot[...].reshape(TILES * PATCH, WIDE),
                    TN,
                ).astype(BF)

            @pl.when((at == 1) & (head >= 1))
            def _():
                stage_core(head - 1)

            @pl.when((at == 2) & (head >= 2))
            def _():
                stage_row(head - 2)

            @pl.when((at == 3) & (head >= 3))
            def _():
                store_qkv(head - 3)

            @pl.when(at == 3)
            def _():
                core_copy(head).start()

        return carry

    lax.fori_loop(0, UNITS + HALF, weight_step, 0)

    for half in range(2):
        columns = slice(half * QKV, (half + 1) * QKV)
        grads[6 + half] = grad_wide[:, columns].reshape(8, 2, 48, QKV)
        core_copy(6 + half).start()

    def d_copy(step):
        lines = pl.ds(pl.multiple_of(lax.rem(my + step, 4) * 32, 32), 32)
        return remote(
            feat_bf.at[:, lines], feat_in.at[step - 1],
            d_send.at[step - 1], d_recv.at[step - 1], x_peer(step),
        )

    feat_bf[...] = feat_acc[...].astype(BF)
    for step in (2, 1, 3):
        d_copy(step).start()
    stage_core(5)
    stage_row(4)
    stage_core(6)
    stage_core(7)
    stage_row(5)
    store_qkv(3)
    store_qkv(4)
    stage_row(6)
    stage_row(7)
    store_qkv(5)
    total = feat_acc[:, mine, :]
    for step in (1, 3, 2):
        d_copy(step).wait_recv()
        total = total + feat_in[step - 1].astype(F32)
    out_feat[...] = total.astype(BF)
    out_out[0, :, :QKV] = stage_high(6)
    out_out[0, :, QKV:] = stage_high(7)

    for step in range(1, 4):
        d_copy(step).wait_send()

    def drain(chunk, carry):
        core_copy(chunk).wait_send()
        z_copy(chunk).wait_send()
        for step in range(1, 4):
            y_copy(chunk, step).wait_send()
        return carry

    lax.fori_loop(0, CHUNKS, drain, 0)

    @pl.when(is_end)
    def _():
        sent = part.at[:, :HALF]
        pltpu.make_async_copy(sent, sent, b_send).wait()
        pltpu.make_async_copy(sent, sent, c_send).wait()

    @pl.when(is_mid)
    def _():
        pltpu.make_async_copy(part, part, b_send).wait()
        pltpu.make_async_copy(part, part, c_send).wait()


def fused(quarter, cot, w_qkv, w_out, mask):
    vmem = pl.BlockSpec(memory_space=pltpu.VMEM)
    dma = pltpu.SemaphoreType.DMA
    units = (HEADS_HERE, TILES, PATCH, UNIT)
    return pl.pallas_call(
        branch,
        out_shape=(
            jax.ShapeDtypeStruct((TILES, 32, WIDE), BF),
            jax.ShapeDtypeStruct((1, 48, HEADS_HERE * QKV), F32),
            jax.ShapeDtypeStruct((1, 48, WIDE), F32),
        ),
        in_specs=[vmem] * 5,
        out_specs=(vmem,) * 3,
        scratch_shapes=[
            pltpu.VMEM((TILES, PATCH, WIDE), BF),
            pltpu.VMEM((WIDE, TILES * PATCH), BF),
            pltpu.VMEM(units, BF),
            pltpu.VMEM(units, BF),
            pltpu.VMEM(units, BF),
            pltpu.VMEM((CHUNKS, 8, 2, 48, QKV), BF),
            pltpu.VMEM((CHUNKS, 8, 48, QKV), BF),
            pltpu.VMEM((CHUNKS, 8, 48, QKV), BF),
            pltpu.VMEM((CHUNKS, 3, 2, 48, QKV), BF),
            pltpu.VMEM((CHUNKS, 2, 48, QKV), BF),
            pltpu.VMEM((CHUNKS, 48, QKV), BF),
            pltpu.VMEM((WIDE, WIDE), BF),
            pltpu.VMEM((TILES, PATCH, WIDE), F32),
            pltpu.VMEM((TILES, PATCH, WIDE), BF),
            pltpu.VMEM((3, TILES, 32, WIDE), BF),
            dma((3,)), dma((3,)),
            dma, dma((HEADS_HERE, TILES)),
            dma, dma((HEADS_HERE, TILES)),
            dma((CHUNKS,)), dma((CHUNKS,)),
            dma((CHUNKS, 3)), dma((CHUNKS, 3)),
            dma((CHUNKS,)), dma((CHUNKS,)),
            dma((3,)), dma((3,)),
        ],
        compiler_params=pltpu.CompilerParams(
            collective_id=0, has_side_effects=True, vmem_limit_bytes=60 * 1024 * 1024
        ),
        cost_estimate=pl.CostEstimate(
            flops=14_000_000_000, bytes_accessed=12_000_000, transcendentals=400_000
        ),
    )(quarter, cot, w_qkv, w_out, mask)


def shards(features, segment_ids, owners, w_qkv, w_out, cotangent):
    me = lax.axis_index("dp")
    my = lax.axis_index("my")
    groups = lax.axis_size("dp")
    own_row = lax.dynamic_slice_in_dim(owners, me, 1, 0)[0]
    positions = jnp.arange(TILES)
    chosen = jnp.sum(
        jnp.where(own_row[None, :] == jnp.arange(groups)[:, None], positions[None, :], 0), axis=1
    )
    quarter = lax.dynamic_slice_in_dim(features, my * 32, 32, 1)
    send_rows = jnp.take(quarter, chosen, axis=0)
    got_rows = lax.all_to_all(send_rows, "dp", split_axis=0, concat_axis=0, tiled=True)
    all_ids = lax.all_gather(segment_ids, "dp", axis=0, tiled=True)
    mine = (owners == me).reshape(-1)
    rank = jnp.cumsum(mine.astype(jnp.int32)) - 1
    listed = jnp.sum(
        jnp.where(
            mine[None, :] & (rank[None, :] == positions[:, None]),
            jnp.arange(groups * TILES)[None, :],
            0,
        ),
        axis=1,
    )
    quarter = jnp.take(got_rows, listed // TILES, axis=0)
    ids = jnp.take(all_ids, listed, axis=0)
    mask = (ids[:, :, None] == ids[:, None, :]).astype(F32)
    return fused(quarter, cotangent, w_qkv, w_out, mask)


def solution(mesh):
    return jax.shard_map(
        shards,
        mesh=mesh,
        in_specs=(
            P("dp", None, "mx"),
            P("dp", None),
            P(),
            P("mx", "my"),
            P("my", "mx"),
            P("dp", None, "mx"),
        ),
        out_specs=(P("dp", "my", "mx"), P("mx", "dp", "my"), P("my", "dp", "mx")),
        check_vma=False,
    )
```

time: 608 us -> 559 us (0.919)
  Pallas kernels: 0 us -> 497 us
  waiting for transfers between devices: 456 us -> 0.01 us
  matrix products: 44.6 us -> 0 us
  blocking collectives: 0 us -> 37.1 us
  starting transfers between devices: 40.4 us -> 12.6 us
  other arithmetic: 26.8 us -> 3.5 us
  local copies, waits for them, and re-layouts: 24.8 us -> 7.67 us
  between operations: 14 us -> 0.78 us
    pallas_call x0 -> x1, Pallas kernels: none -> 497 us  [fused(): pl.pallas_call(branch, out_shape=(jax.ShapeDtypeStruct((TILES, 32, WIDE),...]
    reduce_scatter x4 -> x0, waiting for transfers between devices: 280 us -> none  [the longest x1 98.5 us: shards(): lax.psum_scatter(new_qkv[None].astype(jnp.bfloat16), 'dp', scatter_dimens...]
    all_gather x1 -> x0, waiting for transfers between devices: 121 us -> none  [shards(): shard_rows = lax.all_gather(local_rows, 'mx', axis=0, tiled=True)]
    all_to_all x1, waiting for transfers between devices: 46.1 us -> 0.01 us  [shards(): lax.all_to_all(send_rows, 'dp', split_axis=0, concat_axis=0, tiled=True)]
    dot_general x10 -> x0, matrix products: 41.9 us -> none  [the longest x5 13.4 us: product(): jnp.einsum(pattern, operand_a, operand_b, preferred_element_type=jnp.floa...]
    all_gather x0 -> x1, blocking collectives: none -> 37.1 us  [shards(): all_ids = lax.all_gather(segment_ids, 'dp', axis=0, tiled=True)]
    all_to_all x1 -> x0, starting transfers between devices: 27.3 us -> none  [shards(): lax.all_to_all(send_ids, 'dp', split_axis=0, concat_axis=0, tiled=True)]
    all_to_all x1 -> x0, waiting for transfers between devices: 9.33 us -> none  [shards(): lax.all_to_all(send_ids, 'dp', split_axis=0, concat_axis=0, tiled=True)]
  transfers between devices with their start and end apart: 7 -> 1, of which waited for: 7 -> 0; matrix products, arithmetic and copies ran while one was open for 5% -> 0% of each run, Pallas kernels for 0% -> 0%
where the time goes in v1:
time: 559 us
  Pallas kernels  497 us (89%)
  blocking collectives  37.1 us (7%)
  starting transfers between devices  12.6 us (2%)
  local copies, waits for them, and re-layouts  7.67 us (1%)
    pallas_call x1, Pallas kernels, fused(): pl.pallas_call(branch, out_shape=(jax.ShapeDtypeStruct((TILES, 32, WIDE),...  497 us
    all_gather x1, blocking collectives, shards(): all_ids = lax.all_gather(segment_ids, 'dp', axis=0, tiled=True)  37.1 us
    all_to_all x1, starting transfers between devices, shards(): lax.all_to_all(send_rows, 'dp', split_axis=0, concat_axis=0, tiled=True)  12.6 us
  transfers between devices with their start and end apart: 1, of which 0 were waited for; matrix products, arithmetic and copies ran while one was open for 0% of the time, Pallas kernels for 0%

profile of v1, /device:TPU:1, one launch (start us, length us, event | category | flops | bytes accessed | tf_op | source)
XLA Modules:
  0.0 558.7 jit_solution(855996461555330086)
XLA Ops:
  0.6 0.0 copy-start
  0.7 1.0 dynamic-slice_reduce_fusion
  1.6 0.1 select_reduce_fusion
  1.8 0.3 copy-done
  2.1 0.6 gather_fusion
  2.7 0.0 copy-start.2
  2.7 0.0 copy-start.3
  2.7 1.0 broadcast_select_fusion
  3.8 12.6 %all-to-all-start = ((bf16[16,32,768]{2,1,0:T(8,128)(2,1)}), bf16[16,32,768]{2,1,0:T(8,128)(2,1)S(1)}, u32[]{:S(2)}, u32[]{:S(2)}) async-start(bf16[16,32,768]{2,1,0:T(8,128)(2,1)} %broadcast_select_fusion), calls=%async_computation | async-start | bytes 1572864 | tf_op jit(solution)/shard_map/all_to_all | solution.py:439
  16.4 0.0 copy-done.2
  16.4 0.1 copy.15
  16.5 0.1 and.58
  16.6 0.1 copy.16
  16.6 0.1 reshape.192
  16.7 0.2 reduce-window.8
  16.9 0.0 copy-done.3
  16.9 37.1 %all_gather.3 = s32[128,128]{1,0:T(8,128)S(1)} all-gather(s32[8,128]{1,0:T(8,128)S(1)} %copy-done.3), channel_id=1, replica_groups=mesh['dp'=16,'mx'=4,'my'=4] {'dp'}, dimensions={0}, use_global_device_ids=true | all-gather | bytes 69632 | tf_op jit(solution)/shard_map/all_gather | solution.py:440
  54.0 0.1 add_reduce_fusion
  54.2 0.1 select_reduce_fusion.1
  54.3 0.6 gather_fusion.2
  54.9 0.1 broadcast_select_fusion.2
  55.0 1.0 compare_convert_fusion.mask
  56.0 0.0 all-to-all-done
  56.0 0.6 gather_fusion.1
  56.6 0.8 broadcast_select_fusion.1.quarter
  57.4 497.0 %shard_map.85 = (bf16[8,32,768]{2,1,0:T(8,128)(2,1)}, f32[1,48,2304]{2,1,0:T(8,128)}, f32[1,48,768]{2,1,0:T(8,128)}) custom-call(bf16[8,32,768]{2,1,0:T(8,128)(2,1)} %broadcast_select_fusion.1.quarter, bf16[8,128,768]{2,1,0:T(8,128)(2,1)} %cot.1, bf16[768,2304]{1,0:T(8,128)(2,1)} %w_qkv.1, bf16[768,768]{1,0:T(8,128)(2,1)} %w_out.1, ...), custom_call_target="tpu_custom_call" | custom-call | flops 14000000000 | bytes 12000000 | tf_op jit(solution)/shard_map/pallas_call | solution.py:386
  554.4 0.0 copy-start.1
  554.4 1.8 copy.21
  556.2 1.8 copy.22
  558.0 0.0 copy-done.1
  558.0 0.7 copy.23
  (9 shorter events, 0.1 us)
Async XLA Ops:
  0.6 1.4 copy-start
  2.7 13.7 %copy-start.2 = (s32[16,8]{0,1:T(8,128)S(1)}, s32[16,8]{0,1:T(8,128)}, u32[]{:S(2)}) copy-start(s32[16,8]{0,1:T(8,128)} %param.8) | copy-start | bytes 1540
  2.7 14.2 %copy-start.3 = (s32[8,128]{1,0:T(8,128)S(1)}, s32[8,128]{1,0:T(8,128)}, u32[]{:S(2)}) copy-start(s32[8,128]{1,0:T(8,128)} %param.7) | copy-start | bytes 12292
  3.8 52.2 %all-to-all-start = ((bf16[16,32,768]{2,1,0:T(8,128)(2,1)}), bf16[16,32,768]{2,1,0:T(8,128)(2,1)S(1)}, u32[]{:S(2)}, u32[]{:S(2)}) async-start(bf16[16,32,768]{2,1,0:T(8,128)(2,1)} %broadcast_select_fusion), calls=%async_computation | async-start | bytes 1572864 | tf_op jit(solution)/shard_map/all_to_all | solution.py:439
  554.4 3.6 copy-start.1

commit v2 on v1

--- a/solution.py
+++ b/solution.py
@@ -15,6 +15,9 @@
 QKV = 3 * HEAD
 UNIT = QKV + HEAD
 CHUNKS = 8
+AHEAD = 6
+SLOTS = 2
+LAG = 2
 BF = jnp.bfloat16
 F32 = jnp.float32
 MESH = pl.DeviceIdType.MESH
@@ -72,7 +75,7 @@
     out_feat, out_qkv, out_out,
     feat, feat_t, part, chain, found, grads, core_in, core_sum, y_in, y_sum, z_in,
     grad_wide, feat_acc, feat_bf, feat_in,
-    x_send, x_recv, b_send, b_recv, c_send, c_recv,
+    x_send, x_recv, b_send, b_recv, c_recv,
     core_send, core_recv, y_send, y_recv, z_send, z_recv, d_send, d_recv,
 ):
     dp = lax.axis_index("dp")
@@ -86,6 +89,10 @@
     own = jnp.where(mx == 0, 0, HALF)
     other = HALF - own
     near = jnp.where(mx == 0, 1, 2)
+    middle = 3 - mx
+    edge = jnp.where(mx == 1, 0, 3)
+    edge_base = jnp.where(mx == 1, 0, HALF)
+    far_base = HALF - edge_base
 
     core_peer = (dp + 1 - 2 * core, mx, my)
     high_peer = (row * 4 + (1 - high) * 2 + core, mx, my)
@@ -156,32 +163,63 @@
         part[head, tile, :, QKV:] = back[:PATCH]
         part[head, tile + HALF, :, QKV:] = back[PATCH:]
 
-    def b_copy(head, tile, to):
-        return remote(
-            part.at[head, tile], chain.at[head, tile], b_send, b_recv.at[head, tile], along(to)
-        )
-
-    def c_copy(head, tile, to):
-        return remote(
-            found.at[head, tile], found.at[head, tile], c_send, c_recv.at[head, tile], along(to)
-        )
+    def b_copy(head, tile, to, slot):
+        return remote(
+            part.at[head, tile], chain.at[head, tile],
+            b_send.at[slot], b_recv.at[head, tile], along(to),
+        )
+
+    def c_copy(head, tile, to, slot):
+        return remote(
+            found.at[head, tile], found.at[head, tile],
+            b_send.at[slot], c_recv.at[head, tile], along(to),
+        )
+
+    def slot_of(unit, stream=0):
+        return stream * SLOTS + lax.rem(unit, SLOTS)
+
+    def b_out(unit):
+        return b_copy(unit // HALF, other + lax.rem(unit, HALF), near, slot_of(unit))
+
+    def c_out(unit):
+        return c_copy(unit // HALF, own + lax.rem(unit, HALF), near, slot_of(unit))
+
+    def free(unit, stream=0):
+        b_copy(0, 0, near, slot_of(unit, stream)).wait_send()
 
     @pl.when(is_end)
     def _():
         def send_out(unit, carry):
             project(unit)
-            b_copy(unit // HALF, other + lax.rem(unit, HALF), near).start()
+
+            @pl.when(unit >= SLOTS)
+            def _():
+                free(unit)
+
+            b_out(unit).start()
             return carry
 
-        lax.fori_loop(0, UNITS, send_out, 0)
+        lax.fori_loop(0, AHEAD, send_out, 0)
 
         def finish(unit, carry):
             head = unit // HALF
             tile = own + lax.rem(unit, HALF)
-            b_copy(head, tile, near).wait_recv()
+            b_copy(head, tile, near, 0).wait_recv()
             total = part[head, tile].astype(F32) + chain[head, tile].astype(F32)
             found[head, tile] = attend(total, mask[tile])
-            c_copy(head, tile, near).start()
+            later = unit + AHEAD
+
+            @pl.when(later < UNITS)
+            def _():
+                project(later)
+                free(later)
+                b_out(later).start()
+
+            @pl.when(later >= UNITS)
+            def _():
+                free(later)
+                c_out(later - UNITS).start()
+
             return carry
 
         lax.fori_loop(0, UNITS, finish, 0)
@@ -194,15 +232,28 @@
 
         lax.fori_loop(0, HALF, prepare, 0)
 
+        def add_on(unit, base, to, stream):
+            head = unit // HALF
+            tile = base + lax.rem(unit, HALF)
+            b_copy(head, tile, to, 0).wait_recv()
+            part[head, tile] = (
+                part[head, tile].astype(F32) + chain[head, tile].astype(F32)
+            ).astype(BF)
+
+            @pl.when(unit >= SLOTS)
+            def _():
+                free(unit, stream)
+
+            b_copy(head, tile, to, slot_of(unit, stream)).start()
+
         def pass_on(unit, carry):
-            head = unit // HALF
-            at = lax.rem(unit, HALF)
-            for tile, to in ((at + HALF, mx + 1), (at, mx - 1)):
-                b_copy(head, tile, to).wait_recv()
-                part[head, tile] = (
-                    part[head, tile].astype(F32) + chain[head, tile].astype(F32)
-                ).astype(BF)
-                b_copy(head, tile, to).start()
+            @pl.when(unit < UNITS)
+            def _():
+                add_on(unit, far_base, middle, 0)
+
+            @pl.when(unit >= LAG)
+            def _():
+                add_on(unit - LAG, edge_base, edge, 1)
 
             @pl.when(unit + HALF < UNITS)
             def _():
@@ -210,7 +261,7 @@
 
             return carry
 
-        lax.fori_loop(0, UNITS, pass_on, 0)
+        lax.fori_loop(0, UNITS + LAG, pass_on, 0)
 
     feat_acc[...] = jnp.zeros_like(feat_acc)
 
@@ -256,32 +307,47 @@
         columns = pl.ds(pl.multiple_of(chunk * QKV, HEAD), QKV)
         out_qkv[0, :, columns] = stage_high(chunk)
 
+    def hand_on(unit, base, to, stream):
+        head = unit // HALF
+        tile = base + lax.rem(unit, HALF)
+        c_copy(head, tile, to, 0).wait_recv()
+        free(unit, stream)
+        c_copy(head, tile, to, slot_of(unit, stream)).start()
+
     def weight_step(unit, carry):
-        at = lax.rem(unit, HALF)
-
-        @pl.when(unit < UNITS)
+        @pl.when(is_mid)
         def _():
-            head = unit // HALF
-
-            @pl.when(is_mid)
-            def _():
-                for tile, to in ((at, mx + 1), (at + HALF, mx - 1)):
-                    c_copy(head, tile, to).wait_recv()
-                    c_copy(head, tile, to).start()
-
-            @pl.when(is_end)
-            def _():
-                c_copy(head, other + at, near).wait_recv()
+            @pl.when(unit < UNITS)
+            def _():
+                hand_on(unit, edge_base, middle, 0)
+
+            @pl.when((unit >= LAG) & (unit < UNITS + LAG))
+            def _():
+                hand_on(unit - LAG, far_base, edge, 1)
+
+        @pl.when(is_end)
+        def _():
+            @pl.when(unit + AHEAD < UNITS)
+            def _():
+                free(unit + AHEAD)
+                c_out(unit + AHEAD).start()
+
+            @pl.when((unit >= LAG) & (unit < UNITS + LAG))
+            def _():
+                got = unit - LAG
+                c_copy(got // HALF, other + lax.rem(got, HALF), near, 0).wait_recv()
 
         @pl.when(unit < HALF)
         def _():
             for tile in range(2):
-                columns = pl.ds(pl.multiple_of((2 * at + tile) * PATCH, PATCH), PATCH)
-                feat_t[:, columns] = feat[2 * at + tile].T
-
-        @pl.when(unit >= HALF)
+                columns = pl.ds(pl.multiple_of((2 * unit + tile) * PATCH, PATCH), PATCH)
+                feat_t[:, columns] = feat[2 * unit + tile].T
+
+        @pl.when(unit >= HALF - 1 + LAG)
         def _():
-            head = unit // HALF - 1
+            done = unit - (HALF - 1 + LAG)
+            head = done // HALF
+            at = lax.rem(done, HALF)
             grad = found[head, :, :, HEAD:].reshape(TILES * PATCH, QKV)
             lines = pl.ds(pl.multiple_of(at * 192, 64), 192)
             piece = dot(feat_t[lines, :], grad, NN).astype(BF)
@@ -320,7 +386,7 @@
 
         return carry
 
-    lax.fori_loop(0, UNITS + HALF, weight_step, 0)
+    lax.fori_loop(0, UNITS + HALF - 1 + LAG, weight_step, 0)
 
     for half in range(2):
         columns = slice(half * QKV, (half + 1) * QKV)
@@ -367,16 +433,13 @@
 
     lax.fori_loop(0, CHUNKS, drain, 0)
 
-    @pl.when(is_end)
-    def _():
-        sent = part.at[:, :HALF]
-        pltpu.make_async_copy(sent, sent, b_send).wait()
-        pltpu.make_async_copy(sent, sent, c_send).wait()
+    for slot in range(SLOTS):
+        free(slot)
 
     @pl.when(is_mid)
     def _():
-        pltpu.make_async_copy(part, part, b_send).wait()
-        pltpu.make_async_copy(part, part, c_send).wait()
+        for slot in range(SLOTS):
+            free(slot, 1)
 
 
 def fused(quarter, cot, w_qkv, w_out, mask):
@@ -409,8 +472,7 @@
             pltpu.VMEM((TILES, PATCH, WIDE), BF),
             pltpu.VMEM((3, TILES, 32, WIDE), BF),
             dma((3,)), dma((3,)),
-            dma, dma((HEADS_HERE, TILES)),
-            dma, dma((HEADS_HERE, TILES)),
+            dma((2 * SLOTS,)), dma((HEADS_HERE, TILES)), dma((HEADS_HERE, TILES)),
             dma((CHUNKS,)), dma((CHUNKS,)),
             dma((CHUNKS, 3)), dma((CHUNKS, 3)),
             dma((CHUNKS,)), dma((CHUNKS,)),

time: 559 us -> 269 us (0.48)
  Pallas kernels: 497 us -> 206 us
    pallas_call x1, Pallas kernels: 497 us -> 206 us  [fused(): pl.pallas_call(branch, out_shape=(jax.ShapeDtypeStruct((TILES, 32, WIDE),...]
  transfers between devices with their start and end apart: 1 -> 1, of which waited for: 0 -> 0; matrix products, arithmetic and copies ran while one was open for 0% -> 1% of each run, Pallas kernels for 0% -> 0%
where the time goes in v2:
time: 269 us; the launch traced here: 268 us
  Pallas kernels  206 us (77%)
  blocking collectives  37.1 us (14%)
  starting transfers between devices  12.6 us (5%)
  local copies, waits for them, and re-layouts  7.67 us (3%)
  other arithmetic  3.5 us (1%)
    pallas_call x1, Pallas kernels, fused(): pl.pallas_call(branch, out_shape=(jax.ShapeDtypeStruct((TILES, 32, WIDE),...  206 us
    all_gather x1, blocking collectives, shards(): all_ids = lax.all_gather(segment_ids, 'dp', axis=0, tiled=True)  37.1 us
    all_to_all x1, starting transfers between devices, shards(): lax.all_to_all(send_rows, 'dp', split_axis=0, concat_axis=0, tiled=True)  12.6 us
  transfers between devices with their start and end apart: 1, of which 0 were waited for; matrix products, arithmetic and copies ran while one was open for 1% of the time, Pallas kernels for 0%

profile of v2, /device:TPU:1, one launch (start us, length us, event | category | flops | bytes accessed | tf_op | source)
XLA Modules:
  0.0 268.1 jit_solution(9036417193467622655)
XLA Ops:
  0.6 0.0 copy-start
  0.7 1.0 dynamic-slice_reduce_fusion
  1.6 0.1 select_reduce_fusion
  1.8 0.3 copy-done
  2.1 0.6 gather_fusion
  2.7 0.0 copy-start.2
  2.7 0.0 copy-start.3
  2.7 1.0 broadcast_select_fusion
  3.8 12.6 %all-to-all-start = ((bf16[16,32,768]{2,1,0:T(8,128)(2,1)}), bf16[16,32,768]{2,1,0:T(8,128)(2,1)S(1)}, u32[]{:S(2)}, u32[]{:S(2)}) async-start(bf16[16,32,768]{2,1,0:T(8,128)(2,1)} %broadcast_select_fusion), calls=%async_computation | async-start | bytes 1572864 | tf_op jit(solution)/shard_map/all_to_all | solution.py:501
  16.4 0.0 copy-done.2
  16.4 0.1 copy.15
  16.5 0.1 and.58
  16.6 0.1 copy.16
  16.6 0.1 reshape.192
  16.7 0.2 reduce-window.8
  16.9 0.0 copy-done.3
  16.9 37.1 %all_gather.3 = s32[128,128]{1,0:T(8,128)S(1)} all-gather(s32[8,128]{1,0:T(8,128)S(1)} %copy-done.3), channel_id=1, replica_groups=mesh['dp'=16,'mx'=4,'my'=4] {'dp'}, dimensions={0}, use_global_device_ids=true | all-gather | bytes 69632 | tf_op jit(solution)/shard_map/all_gather | solution.py:502
  54.0 0.1 add_reduce_fusion
  54.2 0.1 select_reduce_fusion.1
  54.3 0.6 gather_fusion.2
  54.9 0.1 broadcast_select_fusion.2
  55.0 1.0 compare_convert_fusion.mask
  56.0 0.0 all-to-all-done
  56.0 0.6 gather_fusion.1
  56.6 0.8 broadcast_select_fusion.1.quarter
  57.4 206.4 %shard_map.85 = (bf16[8,32,768]{2,1,0:T(8,128)(2,1)}, f32[1,48,2304]{2,1,0:T(8,128)}, f32[1,48,768]{2,1,0:T(8,128)}) custom-call(bf16[8,32,768]{2,1,0:T(8,128)(2,1)} %broadcast_select_fusion.1.quarter, bf16[8,128,768]{2,1,0:T(8,128)(2,1)} %cot.1, bf16[768,2304]{1,0:T(8,128)(2,1)} %w_qkv.1, bf16[768,768]{1,0:T(8,128)(2,1)} %w_out.1, ...), custom_call_target="tpu_custom_call" | custom-call | flops 14000000000 | bytes 12000000 | tf_op jit(solution)/shard_map/pallas_call | solution.py:449
  263.8 0.0 copy-start.1
  263.9 1.8 copy.21
  265.7 1.8 copy.22
  267.5 0.0 copy-done.1
  267.5 0.7 copy.23
  (9 shorter events, 0.1 us)
Async XLA Ops:
  0.6 1.4 copy-start
  2.7 13.7 %copy-start.2 = (s32[16,8]{0,1:T(8,128)S(1)}, s32[16,8]{0,1:T(8,128)}, u32[]{:S(2)}) copy-start(s32[16,8]{0,1:T(8,128)} %param.8) | copy-start | bytes 1540
  2.7 14.2 %copy-start.3 = (s32[8,128]{1,0:T(8,128)S(1)}, s32[8,128]{1,0:T(8,128)}, u32[]{:S(2)}) copy-start(s32[8,128]{1,0:T(8,128)} %param.7) | copy-start | bytes 12292
  3.8 52.2 %all-to-all-start = ((bf16[16,32,768]{2,1,0:T(8,128)(2,1)}), bf16[16,32,768]{2,1,0:T(8,128)(2,1)S(1)}, u32[]{:S(2)}, u32[]{:S(2)}) async-start(bf16[16,32,768]{2,1,0:T(8,128)(2,1)} %broadcast_select_fusion), calls=%async_computation | async-start | bytes 1572864 | tf_op jit(solution)/shard_map/all_to_all | solution.py:501
  263.8 3.6 %copy-start.1 = (f32[1,48,768]{2,1,0:T(8,128)S(1)}, f32[1,48,768]{2,1,0:T(8,128)}, u32[]{:S(2)}) copy-start(f32[1,48,768]{2,1,0:T(8,128)} %get-tuple-element.14) | copy-start | bytes 442372

commit v3 on v2

--- a/solution.py
+++ b/solution.py
@@ -10,6 +10,11 @@
 TILES = 8
 HALF = 4
 UNITS = HEADS_HERE * HALF
+GROUPS = HEADS_HERE + 2
+SUMS = GROUPS * HALF
+BACKS = 2 * HALF
+LOADERS = 16
+QUARTER = 32
 PATCH = 128
 WIDE = 768
 QKV = 3 * HEAD
@@ -47,13 +52,12 @@
     )
 
 
-def attend(total, mask):
+def attend(total, grad_bf, mask):
     query_hat, query_inv = normalize(total[:, :HEAD])
     key_hat, key_inv = normalize(total[:, HEAD : 2 * HEAD])
     query_bf = query_hat.astype(BF)
     key_bf = key_hat.astype(BF)
-    value_bf = total[:, 2 * HEAD : 3 * HEAD].astype(BF)
-    grad_bf = total[:, 3 * HEAD :].astype(BF)
+    value_bf = total[:, 2 * HEAD :].astype(BF)
     expo = jnp.exp(dot(query_bf, key_bf, NT) * SCALE) * mask
     weights = expo / jnp.sum(expo, axis=-1, keepdims=True)
     weights_bf = weights.astype(BF)
@@ -71,11 +75,11 @@
 
 
 def branch(
-    quarter, cot, w_qkv, w_out, mask,
+    owners, given, given_ids, cot, w_qkv, w_out,
     out_feat, out_qkv, out_out,
     feat, feat_t, part, chain, found, grads, core_in, core_sum, y_in, y_sum, z_in,
-    grad_wide, feat_acc, feat_bf, feat_in,
-    x_send, x_recv, b_send, b_recv, c_recv,
+    grad_wide, feat_acc, feat_bf, feat_in, outbox, inbox, ids, mask,
+    a_send, a_recv, i_send, i_recv, x_send, x_recv, b_send, b_recv, c_send, c_recv,
     core_send, core_recv, y_send, y_recv, z_send, z_recv, d_send, d_recv,
 ):
     dp = lax.axis_index("dp")
@@ -111,22 +115,24 @@
     def greet(peer):
         pl.semaphore_signal(barrier, inc=1, device_id=peer, device_id_type=MESH)
 
-    greet(core_peer)
-    greet(high_peer)
+    def dp_peer(step):
+        return (lax.rem(dp + step, LOADERS), mx, my)
+
+    for step in range(1, LOADERS):
+        greet(dp_peer(step))
     for step in range(1, 4):
-        greet(row_peer(step))
         greet(x_peer(step))
 
     @pl.when(is_end)
     def _():
         greet(along(near))
-        pl.semaphore_wait(barrier, 9)
+        pl.semaphore_wait(barrier, 19)
 
     @pl.when(is_mid)
     def _():
         greet(along(mx - 1))
         greet(along(mx + 1))
-        pl.semaphore_wait(barrier, 10)
+        pl.semaphore_wait(barrier, 20)
 
     def remote(src, dst, send, recv, peer):
         return pltpu.make_async_remote_copy(
@@ -134,34 +140,103 @@
             device_id=peer, device_id_type=MESH,
         )
 
-    mine = pl.ds(pl.multiple_of(my * 32, 32), 32)
+    mine = pl.ds(pl.multiple_of(my * QUARTER, QUARTER), QUARTER)
+
+    def position(loader, owner):
+        place = jnp.int32(0)
+        for tile in range(TILES):
+            place = jnp.where(owners[loader, tile] == owner, tile, place)
+        return place
+
+    def fill(owner, carry):
+        outbox[owner] = given[position(dp, owner), mine, :]
+        return carry
+
+    lax.fori_loop(0, LOADERS, fill, 0)
+
+    def a_copy(step):
+        return remote(
+            outbox.at[lax.rem(dp + step, LOADERS)], inbox.at[dp],
+            a_send.at[step - 1], a_recv.at[step - 1], dp_peer(step),
+        )
+
+    def i_copy(step):
+        return remote(
+            given_ids, ids.at[dp], i_send.at[step - 1], i_recv.at[step - 1], dp_peer(step)
+        )
+
+    for step in (2, 6, 10, 14, 1, 3, 5, 7, 9, 11, 13, 15, 4, 12, 8):
+        a_copy(step).start()
+        i_copy(step).start()
+    inbox[dp] = outbox[dp]
+    ids[dp] = given_ids[...]
+
+    loaders = [jnp.int32(0)] * TILES
+    places = [jnp.int32(0)] * TILES
+    count = jnp.int32(0)
+    for loader in range(LOADERS):
+        here = jnp.int32(0)
+        for tile in range(TILES):
+            here = jnp.where(owners[loader, tile] == dp, 1, here)
+        place = position(loader, dp)
+        for tile in range(TILES):
+            fits = (here > 0) & (count == tile)
+            loaders[tile] = jnp.where(fits, loader, loaders[tile])
+            places[tile] = jnp.where(fits, place, places[tile])
+        count = count + here
 
     def x_copy(step):
         return remote(
-            quarter, feat.at[:, mine], x_send.at[step - 1], x_recv.at[step - 1], x_peer(step)
-        )
-
-    for step in (2, 1, 3):
-        x_copy(step).start()
-    feat[:, mine, :] = quarter[...]
-    for step in (1, 3, 2):
-        x_copy(step).wait_recv()
-    for step in range(1, 4):
-        x_copy(step).wait_send()
+            feat.at[:, mine], feat.at[:, mine],
+            x_send.at[step - 1], x_recv.at[step - 1], x_peer(step),
+        )
+
+    def take_tiles():
+        for step in range(1, LOADERS):
+            a_copy(step).wait_recv()
+        for tile in range(TILES):
+            feat[tile, mine, :] = inbox[loaders[tile]]
+        for step in (2, 1, 3):
+            x_copy(step).start()
+
+    def take_quarters():
+        for step in (1, 3, 2):
+            x_copy(step).wait_recv()
+
+    def make_masks():
+        for step in range(1, LOADERS):
+            i_copy(step).wait_recv()
+        for tile in range(HALF):
+            loader = jnp.where(mx == 0, loaders[tile], loaders[tile + HALF])
+            place = jnp.where(mx == 0, places[tile], places[tile + HALF])
+            line = ids[loader, pl.ds(place, 1), :].astype(F32)
+            across = jnp.broadcast_to(line, (PATCH, PATCH))
+            mask[tile] = (across == across.T).astype(F32)
+
+    def project_back(unit):
+        half = unit // HALF
+        tile = lax.rem(unit, HALF)
+        rows = jnp.concatenate([cot[tile], cot[tile + HALF]], axis=0)
+        lines = pl.ds(pl.multiple_of(half * QKV, HEAD), QKV)
+        product = dot(rows, w_out[lines, :], NT).astype(BF)
+        part[half, tile] = product[:PATCH]
+        part[half, tile + HALF] = product[PATCH:]
 
     def project(unit):
-        head = unit // HALF
+        group = unit // HALF
         tile = lax.rem(unit, HALF)
         rows = jnp.concatenate([feat[tile], feat[tile + HALF]], axis=0)
-        columns = pl.ds(pl.multiple_of(head * QKV, HEAD), QKV)
+        columns = pl.ds(pl.multiple_of((group - 2) * QKV, HEAD), QKV)
         product = dot(rows, w_qkv[:, columns], NN).astype(BF)
-        rows = jnp.concatenate([cot[tile], cot[tile + HALF]], axis=0)
-        lines = pl.ds(pl.multiple_of(head * HEAD, HEAD), HEAD)
-        back = dot(rows, w_out[lines, :], NT).astype(BF)
-        part[head, tile, :, :QKV] = product[:PATCH]
-        part[head, tile + HALF, :, :QKV] = product[PATCH:]
-        part[head, tile, :, QKV:] = back[:PATCH]
-        part[head, tile + HALF, :, QKV:] = back[PATCH:]
+        part[group, tile] = product[:PATCH]
+        part[group, tile + HALF] = product[PATCH:]
+
+    def run(function, start, stop):
+        def step(unit, carry):
+            function(unit)
+            return carry
+
+        lax.fori_loop(start, stop, step, 0)
 
     def b_copy(head, tile, to, slot):
         return remote(
@@ -172,7 +247,7 @@
     def c_copy(head, tile, to, slot):
         return remote(
             found.at[head, tile], found.at[head, tile],
-            b_send.at[slot], c_recv.at[head, tile], along(to),
+            c_send.at[slot], c_recv.at[head, tile], along(to),
         )
 
     def slot_of(unit, stream=0):
@@ -184,70 +259,85 @@
     def c_out(unit):
         return c_copy(unit // HALF, own + lax.rem(unit, HALF), near, slot_of(unit))
 
-    def free(unit, stream=0):
+    def b_free(unit, stream=0):
         b_copy(0, 0, near, slot_of(unit, stream)).wait_send()
+
+    def c_free(unit, stream=0):
+        c_copy(0, 0, near, slot_of(unit, stream)).wait_send()
 
     @pl.when(is_end)
     def _():
-        def send_out(unit, carry):
-            project(unit)
-
+        run(project_back, 0, BACKS)
+
+        def send_out(unit):
             @pl.when(unit >= SLOTS)
             def _():
-                free(unit)
+                b_free(unit)
 
             b_out(unit).start()
-            return carry
-
-        lax.fori_loop(0, AHEAD, send_out, 0)
-
-        def finish(unit, carry):
-            head = unit // HALF
-            tile = own + lax.rem(unit, HALF)
-            b_copy(head, tile, near, 0).wait_recv()
-            total = part[head, tile].astype(F32) + chain[head, tile].astype(F32)
-            found[head, tile] = attend(total, mask[tile])
+
+        def finish(unit):
+            group = unit // HALF
+            at = lax.rem(unit, HALF)
+            tile = own + at
+            b_copy(group, tile, near, 0).wait_recv()
+            total = part[group, tile].astype(F32) + chain[group, tile].astype(F32)
+
+            @pl.when(unit < BACKS)
+            def _():
+                part[group, tile] = total.astype(BF)
+
+            @pl.when(unit >= BACKS)
+            def _():
+                head = group - 2
+                columns = pl.ds(pl.multiple_of(lax.rem(head, 3) * HEAD, HEAD), HEAD)
+                found[head, tile] = attend(total, part[head // 3, tile, :, columns], mask[at])
+
             later = unit + AHEAD
 
-            @pl.when(later < UNITS)
+            @pl.when((later >= BACKS) & (later < SUMS))
             def _():
                 project(later)
-                free(later)
+
+            @pl.when(later < SUMS)
+            def _():
+                b_free(later)
                 b_out(later).start()
 
-            @pl.when(later >= UNITS)
-            def _():
-                free(later)
-                c_out(later - UNITS).start()
-
-            return carry
-
-        lax.fori_loop(0, UNITS, finish, 0)
+            @pl.when(later >= SUMS + SLOTS)
+            def _():
+                c_free(later - SUMS)
+
+            @pl.when(later >= SUMS)
+            def _():
+                c_out(later - SUMS).start()
+
+        run(send_out, 0, SLOTS)
+        take_tiles()
+        run(send_out, SLOTS, AHEAD)
+        make_masks()
+        run(finish, 0, BACKS - AHEAD)
+        take_quarters()
+        run(finish, BACKS - AHEAD, SUMS)
 
     @pl.when(is_mid)
     def _():
-        def prepare(unit, carry):
-            project(unit)
-            return carry
-
-        lax.fori_loop(0, HALF, prepare, 0)
-
         def add_on(unit, base, to, stream):
-            head = unit // HALF
+            group = unit // HALF
             tile = base + lax.rem(unit, HALF)
-            b_copy(head, tile, to, 0).wait_recv()
-            part[head, tile] = (
-                part[head, tile].astype(F32) + chain[head, tile].astype(F32)
+            b_copy(group, tile, to, 0).wait_recv()
+            part[group, tile] = (
+                part[group, tile].astype(F32) + chain[group, tile].astype(F32)
             ).astype(BF)
 
             @pl.when(unit >= SLOTS)
             def _():
-                free(unit, stream)
-
-            b_copy(head, tile, to, slot_of(unit, stream)).start()
-
-        def pass_on(unit, carry):
-            @pl.when(unit < UNITS)
+                b_free(unit, stream)
+
+            b_copy(group, tile, to, slot_of(unit, stream)).start()
+
+        def pass_on(unit):
+            @pl.when(unit < SUMS)
             def _():
                 add_on(unit, far_base, middle, 0)
 
@@ -255,13 +345,18 @@
             def _():
                 add_on(unit - LAG, edge_base, edge, 1)
 
-            @pl.when(unit + HALF < UNITS)
+            @pl.when((unit >= BACKS) & (unit + HALF < SUMS))
             def _():
                 project(unit + HALF)
 
-            return carry
-
-        lax.fori_loop(0, UNITS + LAG, pass_on, 0)
+        run(project_back, 0, BACKS)
+        take_tiles()
+        run(pass_on, 0, BACKS)
+        take_quarters()
+        run(project, BACKS, BACKS + HALF)
+        run(pass_on, BACKS, SUMS + LAG)
+        for step in range(1, LOADERS):
+            i_copy(step).wait_recv()
 
     feat_acc[...] = jnp.zeros_like(feat_acc)
 
@@ -311,7 +406,11 @@
         head = unit // HALF
         tile = base + lax.rem(unit, HALF)
         c_copy(head, tile, to, 0).wait_recv()
-        free(unit, stream)
+
+        @pl.when(unit >= SLOTS)
+        def _():
+            c_free(unit, stream)
+
         c_copy(head, tile, to, slot_of(unit, stream)).start()
 
     def weight_step(unit, carry):
@@ -329,7 +428,7 @@
         def _():
             @pl.when(unit + AHEAD < UNITS)
             def _():
-                free(unit + AHEAD)
+                c_free(unit + AHEAD)
                 c_out(unit + AHEAD).start()
 
             @pl.when((unit >= LAG) & (unit < UNITS + LAG))
@@ -421,7 +520,11 @@
     out_out[0, :, :QKV] = stage_high(6)
     out_out[0, :, QKV:] = stage_high(7)
 
+    for step in range(1, LOADERS):
+        a_copy(step).wait_send()
+        i_copy(step).wait_send()
     for step in range(1, 4):
+        x_copy(step).wait_send()
         d_copy(step).wait_send()
 
     def drain(chunk, carry):
@@ -434,18 +537,22 @@
     lax.fori_loop(0, CHUNKS, drain, 0)
 
     for slot in range(SLOTS):
-        free(slot)
+        b_free(slot)
+        c_free(slot)
 
     @pl.when(is_mid)
     def _():
         for slot in range(SLOTS):
-            free(slot, 1)
-
-
-def fused(quarter, cot, w_qkv, w_out, mask):
+            b_free(slot, 1)
+            c_free(slot, 1)
+
+
+def shards(features, segment_ids, owners, w_qkv, w_out, cotangent):
     vmem = pl.BlockSpec(memory_space=pltpu.VMEM)
+    smem = pl.BlockSpec(memory_space=pltpu.SMEM)
     dma = pltpu.SemaphoreType.DMA
     units = (HEADS_HERE, TILES, PATCH, UNIT)
+    sums = (GROUPS, TILES, PATCH, QKV)
     return pl.pallas_call(
         branch,
         out_shape=(
@@ -453,13 +560,13 @@
             jax.ShapeDtypeStruct((1, 48, HEADS_HERE * QKV), F32),
             jax.ShapeDtypeStruct((1, 48, WIDE), F32),
         ),
-        in_specs=[vmem] * 5,
+        in_specs=[smem] + [vmem] * 5,
         out_specs=(vmem,) * 3,
         scratch_shapes=[
             pltpu.VMEM((TILES, PATCH, WIDE), BF),
             pltpu.VMEM((WIDE, TILES * PATCH), BF),
-            pltpu.VMEM(units, BF),
-            pltpu.VMEM(units, BF),
+            pltpu.VMEM(sums, BF),
+            pltpu.VMEM(sums, BF),
             pltpu.VMEM(units, BF),
             pltpu.VMEM((CHUNKS, 8, 2, 48, QKV), BF),
             pltpu.VMEM((CHUNKS, 8, 48, QKV), BF),
@@ -470,9 +577,16 @@
             pltpu.VMEM((WIDE, WIDE), BF),
             pltpu.VMEM((TILES, PATCH, WIDE), F32),
             pltpu.VMEM((TILES, PATCH, WIDE), BF),
-            pltpu.VMEM((3, TILES, 32, WIDE), BF),
+            pltpu.VMEM((3, TILES, QUARTER, WIDE), BF),
+            pltpu.VMEM((LOADERS, QUARTER, WIDE), BF),
+            pltpu.VMEM((LOADERS, QUARTER, WIDE), BF),
+            pltpu.VMEM((LOADERS, TILES, PATCH), jnp.int32),
+            pltpu.VMEM((HALF, PATCH, PATCH), F32),
+            dma((LOADERS - 1,)), dma((LOADERS - 1,)),
+            dma((LOADERS - 1,)), dma((LOADERS - 1,)),
             dma((3,)), dma((3,)),
-            dma((2 * SLOTS,)), dma((HEADS_HERE, TILES)), dma((HEADS_HERE, TILES)),
+            dma((2 * SLOTS,)), dma((GROUPS, TILES)),
+            dma((2 * SLOTS,)), dma((HEADS_HERE, TILES)),
             dma((CHUNKS,)), dma((CHUNKS,)),
             dma((CHUNKS, 3)), dma((CHUNKS, 3)),
             dma((CHUNKS,)), dma((CHUNKS,)),
@@ -484,36 +598,7 @@
         cost_estimate=pl.CostEstimate(
             flops=14_000_000_000, bytes_accessed=12_000_000, transcendentals=400_000
         ),
-    )(quarter, cot, w_qkv, w_out, mask)
-
-
-def shards(features, segment_ids, owners, w_qkv, w_out, cotangent):
-    me = lax.axis_index("dp")
-    my = lax.axis_index("my")
-    groups = lax.axis_size("dp")
-    own_row = lax.dynamic_slice_in_dim(owners, me, 1, 0)[0]
-    positions = jnp.arange(TILES)
-    chosen = jnp.sum(
-        jnp.where(own_row[None, :] == jnp.arange(groups)[:, None], positions[None, :], 0), axis=1
-    )
-    quarter = lax.dynamic_slice_in_dim(features, my * 32, 32, 1)
-    send_rows = jnp.take(quarter, chosen, axis=0)
-    got_rows = lax.all_to_all(send_rows, "dp", split_axis=0, concat_axis=0, tiled=True)
-    all_ids = lax.all_gather(segment_ids, "dp", axis=0, tiled=True)
-    mine = (owners == me).reshape(-1)
-    rank = jnp.cumsum(mine.astype(jnp.int32)) - 1
-    listed = jnp.sum(
-        jnp.where(
-            mine[None, :] & (rank[None, :] == positions[:, None]),
-            jnp.arange(groups * TILES)[None, :],
-            0,
-        ),
-        axis=1,
-    )
-    quarter = jnp.take(got_rows, listed // TILES, axis=0)
-    ids = jnp.take(all_ids, listed, axis=0)
-    mask = (ids[:, :, None] == ids[:, None, :]).astype(F32)
-    return fused(quarter, cotangent, w_qkv, w_out, mask)
+    )(owners, features, segment_ids, cotangent, w_qkv, w_out)
 
 
 def solution(mesh):

time: 269 us -> 228 us (0.85)
  blocking collectives: 37.1 us -> 0 us
  Pallas kernels: 206 us -> 221 us
  starting transfers between devices: 12.6 us -> 0 us
  other arithmetic: 3.5 us -> 0 us
    all_gather x1 -> x0, blocking collectives: 37.1 us -> none  [shards(): all_ids = lax.all_gather(segment_ids, 'dp', axis=0, tiled=True)]
    pallas_call x1, Pallas kernels: 206 us -> 221 us  [shards(): pl.pallas_call(branch, out_shape=(jax.ShapeDtypeStruct((TILES, 32, WIDE),...]
    all_to_all x1 -> x0, starting transfers between devices: 12.6 us -> none  [shards(): lax.all_to_all(send_rows, 'dp', split_axis=0, concat_axis=0, tiled=True)]
    unnamed x11 -> x6, local copies, waits for them, and re-layouts: 4.59 us -> 5.63 us
  transfers between devices with their start and end apart: 1 -> 0, of which waited for: 0 -> 0; matrix products, arithmetic and copies ran while one was open for 1% -> 0% of each run, Pallas kernels for 0% -> 0%
where the time goes in v3:
time: 228 us
  Pallas kernels  221 us (97%)
  local copies, waits for them, and re-layouts  5.63 us (2%)
    pallas_call x1, Pallas kernels, shards(): pl.pallas_call(branch, out_shape=(jax.ShapeDtypeStruct((TILES, 32, WIDE),...  221 us
    unnamed x6, local copies, waits for them, and re-layouts  5.63 us

profile of v3, /device:TPU:1, one launch (start us, length us, event | category | flops | bytes accessed | tf_op | source)
XLA Modules:
  0.0 227.7 jit_solution(14270110623391099827)
XLA Ops:
  0.6 1.4 copy.9.owners
  2.0 221.5 %shard_map.85 = (bf16[8,32,768]{2,1,0:T(8,128)(2,1)}, f32[1,48,2304]{2,1,0:T(8,128)}, f32[1,48,768]{2,1,0:T(8,128)}) custom-call(s32[16,8]{1,0:T(8,128)} %copy.9.owners, bf16[8,128,768]{2,1,0:T(8,128)(2,1)} %given.1, s32[8,128]{1,0:T(8,128)} %given_ids.1, bf16[8,128,768]{2,1,0:T(8,128)(2,1)} %cot.1, bf16[768,2304]{1,0:T(8,128)(2,1)} %w_qkv.1, ...), custom_call_target="tpu_custom_call" | custom-call | flops 14000000000 | bytes 12000000 | tf_op jit(solution)/shard_map/pallas_call | solution.py:556
  223.4 0.0 copy-start
  223.5 1.8 copy.13
  225.3 1.8 copy.14
  227.1 0.0 copy-done
  227.1 0.7 copy.15
Async XLA Ops:
  223.4 3.6 %copy-start = (f32[1,48,768]{2,1,0:T(8,128)S(1)}, f32[1,48,768]{2,1,0:T(8,128)}, u32[]{:S(2)}) copy-start(f32[1,48,768]{2,1,0:T(8,128)} %get-tuple-element.8) | copy-start | bytes 442372

commit v4 on v3

v4 whole, which is shorter than its diff:
```python
import jax
import jax.numpy as jnp
from jax import lax
from jax.experimental import pallas as pl
from jax.experimental.pallas import tpu as pltpu
from jax.sharding import PartitionSpec as P

HEAD = 128
HEADS_HERE = 6
TILES = 8
HALF = 4
GROUPS = HEADS_HERE + 2
BACKS = 2 * HALF
LOADERS = 16
QUARTER = 32
PATCH = 128
WIDE = 768
QKV = 3 * HEAD
UNIT = QKV + HEAD
CHUNKS = 8
SLOTS = ((0, 0), (0, 1), (-1, 0), (-2, 0), (1, 0), (1, 1), (2, 1), (-1, 1))
SUM_SENDS = ((4, True), (5, True), (6, True), (2, False), (3, False), (7, False))
ROW_SENDS = (
    (0, 2, True), (1, 7, True), (2, 3, True), (0, 4, False), (1, 5, False), (5, 6, False)
)
BF = jnp.bfloat16
F32 = jnp.float32
MESH = pl.DeviceIdType.MESH
SCALE = HEAD ** (-0.5)


def dot(a, b, contract):
    return lax.dot_general(a, b, ((contract[0], contract[1]), ((), ())), preferred_element_type=F32)


NN = ((1,), (0,))
NT = ((1,), (1,))
TN = ((0,), (0,))


def normalize(values):
    centered = values - jnp.mean(values, axis=-1, keepdims=True)
    inverse = lax.rsqrt(jnp.mean(centered * centered, axis=-1, keepdims=True) + 1e-06)
    return centered * inverse, inverse


def norm_back(grad_hat, normed, inverse):
    return inverse * (
        grad_hat
        - jnp.mean(grad_hat, axis=-1, keepdims=True)
        - normed * jnp.mean(grad_hat * normed, axis=-1, keepdims=True)
    )


def attend(total, grad_bf, mask):
    query_hat, query_inv = normalize(total[:, :HEAD])
    key_hat, key_inv = normalize(total[:, HEAD : 2 * HEAD])
    query_bf = query_hat.astype(BF)
    key_bf = key_hat.astype(BF)
    value_bf = total[:, 2 * HEAD :].astype(BF)
    expo = jnp.exp(dot(query_bf, key_bf, NT) * SCALE) * mask
    weights = expo / jnp.sum(expo, axis=-1, keepdims=True)
    weights_bf = weights.astype(BF)
    attended = dot(weights_bf, value_bf, NN)
    grad_value = dot(weights_bf, grad_bf, TN)
    grad_weights = dot(grad_bf, value_bf, NT)
    grad_scores = (
        weights
        * (grad_weights - jnp.sum(weights * grad_weights, axis=-1, keepdims=True))
        * SCALE
    ).astype(BF)
    grad_query = norm_back(dot(grad_scores, key_bf, NN), query_hat, query_inv)
    grad_key = norm_back(dot(grad_scores, query_bf, TN), key_hat, key_inv)
    return jnp.concatenate([attended, grad_query, grad_key, grad_value], axis=1).astype(BF)


def branch(
    owners, given, given_ids, cot_given, w_qkv, w_out,
    out_feat, out_qkv, out_out,
    feat, cot, feat_t, part, chain, found, grads, core_in, core_sum, y_in, y_sum, z_in,
    grad_wide, feat_acc, feat_bf, feat_in, outbox, inbox, ids, mask,
    stage, back_out, back_in, cross_send, cross_recv, spread_send, spread_recv,
    a_send, a_recv, i_send, i_recv, b_send, b_recv, c_send, c_recv,
    core_send, core_recv, y_send, y_recv, z_send, z_recv, d_send, d_recv,
):
    dp = lax.axis_index("dp")
    mx = lax.axis_index("mx")
    my = lax.axis_index("my")
    core = lax.rem(dp, 2)
    high = lax.rem(dp // 2, 2)
    row = dp // 4
    core_peer = (dp + 1 - 2 * core, mx, my)
    high_peer = (row * 4 + (1 - high) * 2 + core, mx, my)

    def row_peer(step):
        return (lax.rem(row + step, 4) * 4 + lax.rem(dp, 4), mx, my)

    def x_peer(step):
        return (dp, mx, lax.rem(my + step, 4))

    turned = row * 4 + (1 - high) * 2 + core
    right = (jnp.where(mx == 3, turned, dp), lax.rem(mx + 1, 4), my)
    left = (jnp.where(mx == 0, turned, dp), lax.rem(mx + 3, 4), my)

    barrier = pltpu.get_barrier_semaphore()

    def greet(peer):
        pl.semaphore_signal(barrier, inc=1, device_id=peer, device_id_type=MESH)

    def dp_peer(step):
        return (lax.rem(dp + step, LOADERS), mx, my)

    for step in range(1, LOADERS):
        greet(dp_peer(step))
    for step in range(1, 4):
        greet(x_peer(step))

    greet(right)
    greet(left)
    pl.semaphore_wait(barrier, 20)

    def remote(src, dst, send, recv, peer):
        return pltpu.make_async_remote_copy(
            src_ref=src, dst_ref=dst, send_sem=send, recv_sem=recv,
            device_id=peer, device_id_type=MESH,
        )

    mine = pl.ds(pl.multiple_of(my * QUARTER, QUARTER), QUARTER)

    def tile_of(slot):
        ahead, which = SLOTS[slot]
        return 2 * lax.rem(mx + ahead + 4, 4) + which

    def crosses(slot):
        ahead = SLOTS[slot][0]
        return (mx + ahead < 0) | (mx + ahead > 3)

    def cross_copy(kind, slot):
        src = (cot_given.at[tile_of(slot), mine], stage.at[slot], back_out.at[slot])[kind]
        dst = (cot.at[slot, mine], feat.at[slot, mine], back_in.at[slot])[kind]
        return remote(
            src, dst, cross_send.at[kind, slot], cross_recv.at[kind, slot], high_peer
        )

    def spread_copy(kind, slot, step):
        held = (cot, feat)[kind].at[slot, mine]
        return remote(
            held, held, spread_send.at[kind, slot, step - 1],
            spread_recv.at[kind, slot, step - 1], x_peer(step),
        )

    def spread(kind, slot):
        for step in (2, 1, 3):
            spread_copy(kind, slot, step).start()

    def gather(kind, slot):
        for step in (1, 3, 2):
            spread_copy(kind, slot, step).wait_recv()

    for slot in range(2, TILES):
        @pl.when(crosses(slot))
        def _():
            cross_copy(0, slot).start()

    def position(loader, owner):
        place = jnp.int32(0)
        for tile in range(TILES):
            place = jnp.where(owners[loader, tile] == owner, tile, place)
        return place

    def fill(owner, carry):
        outbox[owner] = given[position(dp, owner), mine, :]
        return carry

    lax.fori_loop(0, LOADERS, fill, 0)

    def a_copy(step):
        return remote(
            outbox.at[lax.rem(dp + step, LOADERS)], inbox.at[dp],
            a_send.at[step - 1], a_recv.at[step - 1], dp_peer(step),
        )

    def i_copy(step):
        return remote(
            given_ids, ids.at[dp], i_send.at[step - 1], i_recv.at[step - 1], dp_peer(step)
        )

    for step in (2, 6, 10, 14, 1, 3, 5, 7, 9, 11, 13, 15, 4, 12, 8):
        a_copy(step).start()
        i_copy(step).start()
    inbox[dp] = outbox[dp]
    ids[dp] = given_ids[...]

    loaders = [jnp.int32(0)] * TILES
    places = [jnp.int32(0)] * TILES
    count = jnp.int32(0)
    for loader in range(LOADERS):
        here = jnp.int32(0)
        for tile in range(TILES):
            here = jnp.where(owners[loader, tile] == dp, 1, here)
        place = position(loader, dp)
        for tile in range(TILES):
            fits = (here > 0) & (count == tile)
            loaders[tile] = jnp.where(fits, loader, loaders[tile])
            places[tile] = jnp.where(fits, place, places[tile])
        count = count + here

    for slot in range(TILES):
        @pl.when(jnp.logical_not(crosses(slot)))
        def _():
            cot[slot] = cot_given[tile_of(slot)]

    def by_place(values, ahead, which):
        found_value = values[which]
        for place in range(4):
            found_value = jnp.where(
                lax.rem(mx + ahead + 4, 4) == place, values[2 * place + which], found_value
            )
        return found_value

    def take_tiles():
        for step in range(1, LOADERS):
            a_copy(step).wait_recv()
        for slot in (2, 3, 4, 5, 6, 7, 0, 1):
            loader = by_place(loaders, *SLOTS[slot])

            @pl.when(crosses(slot))
            def _():
                stage[slot] = inbox[loader]
                cross_copy(1, slot).start()

            @pl.when(jnp.logical_not(crosses(slot)))
            def _():
                feat[slot, mine, :] = inbox[loader]
                spread(1, slot)

    def make_masks():
        for step in range(1, LOADERS):
            i_copy(step).wait_recv()
        for tile in range(2):
            loader = by_place(loaders, 0, tile)
            place = by_place(places, 0, tile)
            line = ids[loader, pl.ds(place, 1), :].astype(F32)
            across = jnp.broadcast_to(line, (PATCH, PATCH))
            mask[tile] = (across == across.T).astype(F32)

    def project_back(unit):
        half = unit // HALF
        tile = lax.rem(unit, HALF)
        rows = jnp.concatenate([cot[tile], cot[tile + HALF]], axis=0)
        lines = pl.ds(pl.multiple_of(half * QKV, HEAD), QKV)
        product = dot(rows, w_out[lines, :], NT).astype(BF)
        part[half, tile] = product[:PATCH]
        part[half, tile + HALF] = product[PATCH:]

    def project(unit):
        group = unit // HALF
        tile = lax.rem(unit, HALF)
        rows = jnp.concatenate([feat[tile], feat[tile + HALF]], axis=0)
        columns = pl.ds(pl.multiple_of((group - 2) * QKV, HEAD), QKV)
        product = dot(rows, w_qkv[:, columns], NN).astype(BF)
        part[group, tile] = product[:PATCH]
        part[group, tile + HALF] = product[PATCH:]

    def run(function, start, stop):
        def step(unit, carry):
            function(unit)
            return carry

        lax.fori_loop(start, stop, step, 0)

    def b_copy(group, which):
        slot, to_right = SUM_SENDS[which]
        return remote(
            part.at[group, slot], chain.at[group, which],
            b_send.at[group, which], b_recv.at[group, which], right if to_right else left,
        )

    def c_copy(head, which):
        slot, there, to_right = ROW_SENDS[which]
        return remote(
            found.at[head, slot], found.at[head, there],
            c_send.at[head, which], c_recv.at[head, which], right if to_right else left,
        )

    def b_first(group):
        for which in (2, 4, 0, 5):
            b_copy(group, which).start()

    def b_forward(group):
        for come, slot, go in ((2, 5, 1), (4, 2, 3)):
            b_copy(group, come).wait_recv()
            part[group, slot] = (
                part[group, slot].astype(F32) + chain[group, come].astype(F32)
            ).astype(BF)
            b_copy(group, go).start()

    def b_total(group, tile):
        total = part[group, tile].astype(F32)
        for come in ((0, 3), (1, 5))[tile]:
            b_copy(group, come).wait_recv()
            total = total + chain[group, come].astype(F32)
        return total

    def c_first(head):
        for which in (0, 4, 3, 1):
            c_copy(head, which).start()

    def c_forward(head):
        for come, go in ((0, 2), (4, 5)):
            c_copy(head, come).wait_recv()
            c_copy(head, go).start()

    def c_finish(head):
        for which in (1, 2, 3, 5):
            c_copy(head, which).wait_recv()

    def attend_head(head):
        columns = pl.ds(pl.multiple_of(lax.rem(head, 3) * HEAD, HEAD), HEAD)
        totals = [b_total(head + 2, tile) for tile in range(2)]
        for tile in range(2):
            found[head, tile] = attend(
                totals[tile], part[head // 3, tile, :, columns], mask[tile]
            )
        c_first(head)

    for slot in range(2, TILES):
        @pl.when(crosses(slot))
        def _():
            cross_copy(0, slot).wait_recv()
            spread(0, slot)

    for slot in range(2, TILES):
        @pl.when(crosses(slot))
        def _():
            gather(0, slot)

    run(project_back, 0, BACKS)
    for group in range(2):
        b_first(group)
    take_tiles()
    for slot in range(2, TILES):
        @pl.when(crosses(slot))
        def _():
            cross_copy(1, slot).wait_recv()
            spread(1, slot)

    make_masks()
    for group in range(2):
        b_forward(group)
    for slot in range(TILES):
        gather(1, slot)
    run(project, BACKS, BACKS + HALF)
    b_first(2)
    for group in range(2):
        for tile in range(2):
            part[group, tile] = b_total(group, tile).astype(BF)

    feat_acc[...] = jnp.zeros_like(feat_acc)

    def core_copy(chunk):
        return remote(
            grads.at[chunk, :, 1 - core], core_in.at[chunk],
            core_send.at[chunk], core_recv.at[chunk], core_peer,
        )

    def y_copy(chunk, step):
        return remote(
            core_sum.at[chunk, pl.ds(2 * lax.rem(row + step, 4), 2)], y_in.at[chunk, step - 1],
            y_send.at[chunk, step - 1], y_recv.at[chunk, step - 1], row_peer(step),
        )

    def z_copy(chunk):
        return remote(
            y_sum.at[chunk, 1 - high], z_in.at[chunk],
            z_send.at[chunk], z_recv.at[chunk], high_peer,
        )

    def stage_core(chunk):
        core_copy(chunk).wait_recv()
        core_sum[chunk] = (
            grads[chunk, :, core].astype(F32) + core_in[chunk].astype(F32)
        ).astype(BF)
        for step in (2, 1, 3):
            y_copy(chunk, step).start()

    def stage_row(chunk):
        total = core_sum[chunk, pl.ds(2 * row, 2)].astype(F32)
        for step in (1, 3, 2):
            y_copy(chunk, step).wait_recv()
            total = total + y_in[chunk, step - 1].astype(F32)
        y_sum[chunk] = total.astype(BF)
        z_copy(chunk).start()

    def stage_high(chunk):
        z_copy(chunk).wait_recv()
        return (y_sum[chunk, high].astype(F32) + z_in[chunk].astype(F32)) * (1.0 / 16.0)

    def store_qkv(chunk):
        columns = pl.ds(pl.multiple_of(chunk * QKV, HEAD), QKV)
        out_qkv[0, :, columns] = stage_high(chunk)

    def weight_piece(head, at):
        grad = found[head, :, :, HEAD:].reshape(TILES * PATCH, QKV)
        lines = pl.ds(pl.multiple_of(at * 192, 64), 192)
        piece = dot(feat_t[lines, :], grad, NN).astype(BF)
        grads[head, pl.ds(2 * at, 2)] = piece.reshape(2, 2, 48, QKV)
        tiles = pl.ds(2 * at, 2)
        columns = pl.ds(pl.multiple_of(head * QKV, HEAD), QKV)
        back = dot(found[head, tiles, :, HEAD:].reshape(2 * PATCH, QKV), w_qkv[:, columns], NT)
        feat_acc[tiles] += back.reshape(2, PATCH, WIDE)

    def weights(head):
        run(lambda at: weight_piece(head, at), 0, 4)
        core_copy(head).start()
        lines = pl.ds(pl.multiple_of(head * HEAD, HEAD), HEAD)
        grad_wide[lines, :] = dot(
            found[head, :, :, :HEAD].reshape(TILES * PATCH, HEAD),
            cot[...].reshape(TILES * PATCH, WIDE),
            TN,
        ).astype(BF)

    def when(least, head, function):
        @pl.when((head >= least) & (head < HEADS_HERE))
        def _():
            function(head)

    def head_step(now):
        when(1, now, lambda head: b_first(head + 2))
        when(0, now - 1, lambda head: b_forward(head + 2))
        when(0, now - 3, c_forward)
        when(1, now + 1, lambda head: run(project, BACKS + HALF * head, BACKS + HALF * head + HALF))
        when(0, now - 2, attend_head)

        @pl.when(now < 4)
        def _():
            for tile in range(2):
                columns = pl.ds(pl.multiple_of((2 * now + tile) * PATCH, PATCH), PATCH)
                feat_t[:, columns] = feat[2 * now + tile].T

        when(0, now - 4, c_finish)
        when(0, now - 4, weights)

        @pl.when(now >= 5)
        def _():
            stage_core(now - 5)

        @pl.when(now >= 6)
        def _():
            stage_row(now - 6)

        @pl.when(now >= 7)
        def _():
            store_qkv(now - 7)

    run(head_step, 0, HEADS_HERE + 4)

    for half in range(2):
        columns = slice(half * QKV, (half + 1) * QKV)
        grads[6 + half] = grad_wide[:, columns].reshape(8, 2, 48, QKV)
        core_copy(6 + half).start()

    def d_copy(step):
        lines = pl.ds(pl.multiple_of(lax.rem(my + step, 4) * 32, 32), 32)
        return remote(
            feat_bf.at[:, lines], feat_in.at[step - 1],
            d_send.at[step - 1], d_recv.at[step - 1], x_peer(step),
        )

    feat_bf[...] = feat_acc[...].astype(BF)
    for step in (2, 1, 3):
        d_copy(step).start()
    stage_core(5)
    stage_row(4)
    stage_core(6)
    stage_core(7)
    stage_row(5)
    store_qkv(3)
    store_qkv(4)
    stage_row(6)
    for step in (1, 3, 2):
        d_copy(step).wait_recv()
    for slot in (2, 3, 4, 5, 6, 7, 0, 1):
        total = feat_acc[slot, mine, :]
        for step in (1, 3, 2):
            total = total + feat_in[step - 1, slot].astype(F32)
        total = total.astype(BF)

        @pl.when(crosses(slot))
        def _():
            back_out[slot] = total
            cross_copy(2, slot).start()

        @pl.when(jnp.logical_not(crosses(slot)))
        def _():
            out_feat[tile_of(slot)] = total

    stage_row(7)
    store_qkv(5)
    out_out[0, :, :QKV] = stage_high(6)
    out_out[0, :, QKV:] = stage_high(7)
    for slot in range(2, TILES):
        @pl.when(crosses(slot))
        def _():
            cross_copy(2, slot).wait_recv()
            out_feat[tile_of(slot)] = back_in[slot]

    for step in range(1, LOADERS):
        a_copy(step).wait_send()
        i_copy(step).wait_send()
    for step in range(1, 4):
        d_copy(step).wait_send()
    for slot in range(TILES):
        @pl.when(crosses(slot))
        def _():
            for kind in range(3):
                cross_copy(kind, slot).wait_send()
            for step in range(1, 4):
                spread_copy(0, slot, step).wait_send()

        for step in range(1, 4):
            spread_copy(1, slot, step).wait_send()

    def drain(chunk, carry):
        core_copy(chunk).wait_send()
        z_copy(chunk).wait_send()
        for step in range(1, 4):
            y_copy(chunk, step).wait_send()
        return carry

    lax.fori_loop(0, CHUNKS, drain, 0)

    def drain_group(group):
        for which in range(6):
            b_copy(group, which).wait_send()

    def drain_head(head):
        for which in range(6):
            c_copy(head, which).wait_send()

    run(drain_group, 0, GROUPS)
    run(drain_head, 0, HEADS_HERE)


def shards(features, segment_ids, owners, w_qkv, w_out, cotangent):
    vmem = pl.BlockSpec(memory_space=pltpu.VMEM)
    smem = pl.BlockSpec(memory_space=pltpu.SMEM)
    dma = pltpu.SemaphoreType.DMA
    units = (HEADS_HERE, TILES, PATCH, UNIT)
    sums = (GROUPS, TILES, PATCH, QKV)
    return pl.pallas_call(
        branch,
        out_shape=(
            jax.ShapeDtypeStruct((TILES, 32, WIDE), BF),
            jax.ShapeDtypeStruct((1, 48, HEADS_HERE * QKV), F32),
            jax.ShapeDtypeStruct((1, 48, WIDE), F32),
        ),
        in_specs=[smem] + [vmem] * 5,
        out_specs=(vmem,) * 3,
        scratch_shapes=[
            pltpu.VMEM((TILES, PATCH, WIDE), BF),
            pltpu.VMEM((TILES, PATCH, WIDE), BF),
            pltpu.VMEM((WIDE, TILES * PATCH), BF),
            pltpu.VMEM(sums, BF),
            pltpu.VMEM((GROUPS, 6, PATCH, QKV), BF),
            pltpu.VMEM(units, BF),
            pltpu.VMEM((CHUNKS, 8, 2, 48, QKV), BF),
            pltpu.VMEM((CHUNKS, 8, 48, QKV), BF),
            pltpu.VMEM((CHUNKS, 8, 48, QKV), BF),
            pltpu.VMEM((CHUNKS, 3, 2, 48, QKV), BF),
            pltpu.VMEM((CHUNKS, 2, 48, QKV), BF),
            pltpu.VMEM((CHUNKS, 48, QKV), BF),
            pltpu.VMEM((WIDE, WIDE), BF),
            pltpu.VMEM((TILES, PATCH, WIDE), F32),
            pltpu.VMEM((TILES, PATCH, WIDE), BF),
            pltpu.VMEM((3, TILES, QUARTER, WIDE), BF),
            pltpu.VMEM((LOADERS, QUARTER, WIDE), BF),
            pltpu.VMEM((LOADERS, QUARTER, WIDE), BF),
            pltpu.VMEM((LOADERS, TILES, PATCH), jnp.int32),
            pltpu.VMEM((2, PATCH, PATCH), F32),
            pltpu.VMEM((TILES, QUARTER, WIDE), BF),
            pltpu.VMEM((TILES, QUARTER, WIDE), BF),
            pltpu.VMEM((TILES, QUARTER, WIDE), BF),
            dma((3, TILES)), dma((3, TILES)),
            dma((2, TILES, 3)), dma((2, TILES, 3)),
            dma((LOADERS - 1,)), dma((LOADERS - 1,)),
            dma((LOADERS - 1,)), dma((LOADERS - 1,)),
            dma((GROUPS, 6)), dma((GROUPS, 6)),
            dma((HEADS_HERE, 6)), dma((HEADS_HERE, 6)),
            dma((CHUNKS,)), dma((CHUNKS,)),
            dma((CHUNKS, 3)), dma((CHUNKS, 3)),
            dma((CHUNKS,)), dma((CHUNKS,)),
            dma((3,)), dma((3,)),
        ],
        compiler_params=pltpu.CompilerParams(
            collective_id=0, has_side_effects=True, vmem_limit_bytes=60 * 1024 * 1024
        ),
        cost_estimate=pl.CostEstimate(
            flops=14_000_000_000, bytes_accessed=12_000_000, transcendentals=400_000
        ),
    )(owners, features, segment_ids, cotangent, w_qkv, w_out)


def solution(mesh):
    return jax.shard_map(
        shards,
        mesh=mesh,
        in_specs=(
            P("dp", None, "mx"),
            P("dp", None),
            P(),
            P("mx", "my"),
            P("my", "mx"),
            P("dp", None, "mx"),
        ),
        out_specs=(P("dp", "my", "mx"), P("mx", "dp", "my"), P("my", "dp", "mx")),
        check_vma=False,
    )
```

time: 228 us -> 199 us (0.87); the launches traced: 228 us -> 196 us
  Pallas kernels: 221 us -> 190 us
    pallas_call x1, Pallas kernels: 221 us -> 190 us  [shards(): pl.pallas_call(branch, out_shape=(jax.ShapeDtypeStruct((TILES, 32, WIDE),...]
where the time goes in v4:
time: 199 us; the launch traced here: 196 us
  Pallas kernels  190 us (95%)
  local copies, waits for them, and re-layouts  5.63 us (3%)
    pallas_call x1, Pallas kernels, shards(): pl.pallas_call(branch, out_shape=(jax.ShapeDtypeStruct((TILES, 32, WIDE),...  190 us
    unnamed x6, local copies, waits for them, and re-layouts  5.63 us

profile of v4, /device:TPU:1, one launch (start us, length us, event | category | flops | bytes accessed | tf_op | source)
XLA Modules:
  0.0 196.4 jit_solution(9398239200499235482)
XLA Ops:
  0.6 1.4 copy.9.owners
  2.0 190.1 %shard_map.85 = (bf16[8,32,768]{2,1,0:T(8,128)(2,1)}, f32[1,48,2304]{2,1,0:T(8,128)}, f32[1,48,768]{2,1,0:T(8,128)}) custom-call(s32[16,8]{1,0:T(8,128)} %copy.9.owners, bf16[8,128,768]{2,1,0:T(8,128)(2,1)} %given.1, s32[8,128]{1,0:T(8,128)} %given_ids.1, bf16[8,128,768]{2,1,0:T(8,128)(2,1)} %cot_given.1, bf16[768,2304]{1,0:T(8,128)(2,1)} %w_qkv.1, ...), custom_call_target="tpu_custom_call" | custom-call | flops 14000000000 | bytes 12000000 | tf_op jit(solution)/shard_map/pallas_call | solution.py:551
  192.1 0.0 copy-start
  192.1 1.8 copy.13
  193.9 1.8 copy.14
  195.7 0.0 copy-done
  195.7 0.7 copy.15
Async XLA Ops:
  192.1 3.6 %copy-start = (f32[1,48,768]{2,1,0:T(8,128)S(1)}, f32[1,48,768]{2,1,0:T(8,128)}, u32[]{:S(2)}) copy-start(f32[1,48,768]{2,1,0:T(8,128)} %get-tuple-element.8) | copy-start | bytes 442372

commit v5 on v4

v5 whole, which is shorter than its diff:
```python
import jax
import jax.numpy as jnp
from jax import lax
from jax.experimental import pallas as pl
from jax.experimental.pallas import tpu as pltpu
from jax.sharding import PartitionSpec as P

HEAD = 128
HEADS_HERE = 6
TILES = 8
HALF = 2
HELD = 4
BOTH = 2 * 768
PIECE = 96
GROUPS = HEADS_HERE + 2
BACKS = 2 * HALF
LOADERS = 16
QUARTER = 32
PATCH = 128
WIDE = 768
QKV = 3 * HEAD
UNIT = QKV + HEAD
CHUNKS = HEADS_HERE
HALF_ROWS = 384
SLOTS = ((0, 0), (0, 1), (-1, 0), (1, 1))


def routes():
    table = {}
    for block in range(4):
        for place in range(4):
            for which in range(2):
                off = 0 if (place - block) % 2 == 0 else 1 - 2 * which
                to = place + off
                slot = which if off == 0 else 2 + which
                table.setdefault((slot, int(to % 4 != block)), {})[block] = (
                    2 * place + which, int(not 0 <= to <= 3)
                )
    return table


ROUTES = routes()
MOVED = tuple((slot, block) for block in (1, 0) for slot in range(4))
WAVES = 2
WAVE = WIDE // WAVES
BF = jnp.bfloat16
F32 = jnp.float32
MESH = pl.DeviceIdType.MESH
SCALE = HEAD ** (-0.5)


def dot(a, b, contract):
    return lax.dot_general(a, b, ((contract[0], contract[1]), ((), ())), preferred_element_type=F32)


NN = ((1,), (0,))
NT = ((1,), (1,))
TN = ((0,), (0,))


def normalize(values):
    centered = values - jnp.mean(values, axis=-1, keepdims=True)
    inverse = lax.rsqrt(jnp.mean(centered * centered, axis=-1, keepdims=True) + 1e-06)
    return centered * inverse, inverse


def norm_back(grad_hat, normed, inverse):
    return inverse * (
        grad_hat
        - jnp.mean(grad_hat, axis=-1, keepdims=True)
        - normed * jnp.mean(grad_hat * normed, axis=-1, keepdims=True)
    )


def attend(total, grad_bf, mask):
    query_hat, query_inv = normalize(total[:, :HEAD])
    key_hat, key_inv = normalize(total[:, HEAD : 2 * HEAD])
    query_bf = query_hat.astype(BF)
    key_bf = key_hat.astype(BF)
    value_bf = total[:, 2 * HEAD :].astype(BF)
    expo = jnp.exp(dot(query_bf, key_bf, NT) * SCALE) * mask
    weights = expo / jnp.sum(expo, axis=-1, keepdims=True)
    weights_bf = weights.astype(BF)
    attended = dot(weights_bf, value_bf, NN)
    grad_value = dot(weights_bf, grad_bf, TN)
    grad_weights = dot(grad_bf, value_bf, NT)
    grad_scores = (
        weights
        * (grad_weights - jnp.sum(weights * grad_weights, axis=-1, keepdims=True))
        * SCALE
    ).astype(BF)
    grad_query = norm_back(dot(grad_scores, key_bf, NN), query_hat, query_inv)
    grad_key = norm_back(dot(grad_scores, query_bf, TN), key_hat, key_inv)
    return jnp.concatenate([attended, grad_query, grad_key, grad_value], axis=1).astype(BF)


def branch(
    owners, features, given_ids, cot_given, w_qkv_given, w_out_given,
    out_feat, out_qkv, out_out,
    given, w_qkv, w_out, load_sem, feat, cot, feat_t, part, chain, found, grads, core_in, core_sum, y_in, y_sum, z_in,
    half_grad, half_in, half_sum, half_y, half_ysum, half_z, grad_wide, feat_acc, feat_bf, feat_in, outbox, inbox_first, inbox_second, ids, mask,
    w_far_send, w_far_recv, w_row_send, w_row_recv, w_core_send, w_core_recv,
    stage, back_out, back_in, cross_send, cross_recv, spread_send, spread_recv,
    a_send, a_recv, i_send, i_recv, b_send, b_recv, c_send, c_recv,
    half_core_send, half_core_recv, half_row_send, half_row_recv, half_high_send, half_high_recv,
    core_send, core_recv, y_send, y_recv, z_send, z_recv, d_send, d_recv,
):
    inbox = (inbox_first, inbox_second)
    dp = lax.axis_index("dp")
    mx = lax.axis_index("mx")
    my = lax.axis_index("my")
    core = lax.rem(dp, 2)
    high = lax.rem(dp // 2, 2)
    row = dp // 4
    core_peer = (dp + 1 - 2 * core, mx, my)
    high_peer = (row * 4 + (1 - high) * 2 + core, mx, my)

    def row_peer(step):
        return (lax.rem(row + step, 4) * 4 + lax.rem(dp, 4), mx, my)

    def x_peer(step):
        return (dp, mx, lax.rem(my + step, 4))

    turned = row * 4 + (1 - high) * 2 + core
    right = (jnp.where(mx == 3, turned, dp), lax.rem(mx + 1, 4), my)
    left = (jnp.where(mx == 0, turned, dp), lax.rem(mx + 3, 4), my)

    mine = pl.ds(pl.multiple_of(my * QUARTER, QUARTER), QUARTER)
    loads = (
        pltpu.make_async_copy(features.at[:, mine], given, load_sem.at[0]),
        pltpu.make_async_copy(w_out_given, w_out.at[:, :WIDE], load_sem.at[1]),
        pltpu.make_async_copy(w_qkv_given, w_qkv.at[:WIDE], load_sem.at[2]),
    )
    for load in loads:
        load.start()

    barrier = pltpu.get_barrier_semaphore()

    def greet(peer):
        pl.semaphore_signal(barrier, inc=1, device_id=peer, device_id_type=MESH)

    def dp_peer(step):
        return (lax.rem(dp + step, LOADERS), mx, my)

    for step in range(1, LOADERS):
        greet(dp_peer(step))
    for step in range(1, 4):
        greet(x_peer(step))

    greet(right)
    greet(left)
    greet((dp, lax.rem(mx + 2, 4), my))
    greet((turned, lax.rem(mx + 2, 4), my))
    def remote(src, dst, send, recv, peer):
        return pltpu.make_async_remote_copy(
            src_ref=src, dst_ref=dst, send_sem=send, recv_sem=recv,
            device_id=peer, device_id_type=MESH,
        )

    def tile_of(slot):
        ahead, which = SLOTS[slot]
        return 2 * lax.rem(mx + ahead + 4, 4) + which

    def crosses(slot):
        ahead = SLOTS[slot][0]
        return (mx + ahead < 0) | (mx + ahead > 3)

    def moves(slot, block):
        return (mx >= 0) if block else crosses(slot)

    def by_block(slot, block, values):
        chosen = values(0, 0)
        for source, (tile, turn) in ROUTES[slot, block].items():
            chosen = jnp.where(mx == source, values(tile, turn), chosen)
        return chosen

    def sent_tile(slot, block):
        return by_block(slot, block, lambda tile, turn: jnp.int32(tile))

    def opposite(block):
        return lax.rem(mx + 2 * block, 4)

    def sent_peer(slot, block):
        turn = by_block(slot, block, lambda tile, turn: jnp.int32(turn))
        return (jnp.where(turn == 1, turned, dp), opposite(block), my)

    def wave_of(kind, block):
        return pl.ds(block * WIDE + kind * WAVE, WAVE)

    def block_of(block):
        return pl.ds(block * WIDE, WIDE)

    def cross_copy(kind, slot, block):
        if kind < WAVES:
            src, dst = stage.at[kind, block, slot], feat.at[slot, mine, wave_of(kind, block)]
        else:
            src = cot_given.at[sent_tile(slot, block), mine]
            dst = cot.at[slot, mine, block_of(block)]
        return remote(
            src, dst, cross_send.at[kind, slot, block], cross_recv.at[kind, slot, block],
            sent_peer(slot, block),
        )

    def return_copy(slot, block):
        peer = (jnp.where(crosses(slot), turned, dp), opposite(block), my)
        return remote(
            back_out.at[slot, block], back_in.at[slot, block],
            cross_send.at[WAVES + 1, slot, block], cross_recv.at[WAVES + 1, slot, block], peer,
        )

    def spread_copy(kind, slot, block, step):
        if kind < WAVES:
            held = feat.at[slot, mine, wave_of(kind, block)]
        else:
            held = cot.at[slot, mine, block_of(block)]
        return remote(
            held, held, spread_send.at[kind, slot, block, step - 1],
            spread_recv.at[kind, slot, block, step - 1], x_peer(step),
        )

    def spread(kind, slot, block):
        for step in (2, 1, 3):
            spread_copy(kind, slot, block, step).start()

    def gather(kind, slot, block):
        for step in (1, 3, 2):
            spread_copy(kind, slot, block, step).wait_recv()

    def cot_load(slot):
        return pltpu.make_async_copy(
            cot_given.at[tile_of(slot)], cot.at[slot, :, block_of(0)], load_sem.at[3 + slot]
        )

    for slot in range(HELD):
        @pl.when(jnp.logical_not(crosses(slot)))
        def _():
            cot_load(slot).start()

    def weight_part(kind, index):
        lines = pl.ds(pl.multiple_of(index * PIECE, PIECE), PIECE)
        if kind == 0:
            return w_out.at[lines, block_of(1)]
        return w_qkv.at[pl.ds(pl.multiple_of(WIDE + index * PIECE, PIECE), PIECE)]

    own_part = 2 * row + core

    def w_far_copy(kind):
        lines = pl.ds(pl.multiple_of(own_part * PIECE, PIECE), PIECE)
        peer = (jnp.where(lax.rem(row, 2) == 0, dp, turned), opposite(1), my)
        return remote(
            (w_out_given, w_qkv_given)[kind].at[lines], weight_part(kind, own_part),
            w_far_send.at[kind], w_far_recv.at[kind], peer,
        )

    def w_row_copy(kind, step):
        held = weight_part(kind, own_part)
        return remote(
            held, held, w_row_send.at[kind, step - 1], w_row_recv.at[kind, step - 1],
            row_peer(step),
        )

    def w_core_copy(kind, step):
        held = weight_part(kind, 2 * lax.rem(row - step + 4, 4) + core)
        return remote(
            held, held, w_core_send.at[kind, step], w_core_recv.at[kind, step], core_peer
        )

    def w_spread(kind):
        w_far_copy(kind).wait_recv()
        for step in (2, 1, 3):
            w_row_copy(kind, step).start()
        w_core_copy(kind, 0).start()

    def w_share(kind):
        for step in (1, 3, 2):
            w_row_copy(kind, step).wait_recv()
            w_core_copy(kind, step).start()

    def w_wait(kind):
        for step in (0, 1, 3, 2):
            w_core_copy(kind, step).wait_recv()

    def position(loader, owner):
        place = jnp.int32(0)
        for tile in range(TILES):
            place = jnp.where(owners[loader, tile] == owner, tile, place)
        return place

    loads[0].wait()

    def fill(owner, carry):
        tile = position(dp, owner)
        for wave in range(WAVES):
            outbox[wave, owner] = given[tile, :, wave * WAVE : (wave + 1) * WAVE]
        return carry

    lax.fori_loop(0, LOADERS, fill, 0)

    def a_copy(wave, step):
        return remote(
            outbox.at[wave, lax.rem(dp + step, LOADERS)], inbox[wave].at[dp],
            a_send.at[wave, step - 1], a_recv.at[wave, step - 1], dp_peer(step),
        )

    def i_copy(step):
        return remote(
            given_ids, ids.at[dp], i_send.at[step - 1], i_recv.at[step - 1], dp_peer(step)
        )

    def send_wave(wave):
        for step in (2, 6, 10, 14, 1, 3, 5, 7, 9, 11, 13, 15, 4, 12, 8):
            a_copy(wave, step).start()

    for wave in range(WAVES):
        inbox[wave][dp] = outbox[wave, dp]
    ids[dp] = given_ids[...]
    pl.semaphore_wait(barrier, 22)
    for slot, block in MOVED:
        @pl.when(moves(slot, block))
        def _():
            cross_copy(WAVES, slot, block).start()

    w_far_copy(0).start()
    send_wave(0)
    w_far_copy(1).start()
    send_wave(1)
    for step in range(1, LOADERS):
        i_copy(step).start()

    loaders = [jnp.int32(0)] * TILES
    places = [jnp.int32(0)] * TILES
    count = jnp.int32(0)
    for loader in range(LOADERS):
        here = jnp.int32(0)
        for tile in range(TILES):
            here = jnp.where(owners[loader, tile] == dp, 1, here)
        place = position(loader, dp)
        for tile in range(TILES):
            fits = (here > 0) & (count == tile)
            loaders[tile] = jnp.where(fits, loader, loaders[tile])
            places[tile] = jnp.where(fits, place, places[tile])
        count = count + here

    def by_place(values, ahead, which):
        found_value = values[which]
        for place in range(4):
            found_value = jnp.where(
                lax.rem(mx + ahead + 4, 4) == place, values[2 * place + which], found_value
            )
        return found_value

    def picked(slot, block):
        return by_block(slot, block, lambda tile, turn: loaders[tile])

    def take_wave(wave):
        for step in range(1, LOADERS):
            a_copy(wave, step).wait_recv()
        if wave + 2 < WAVES:
            send_wave(wave + 2)
        for slot, block in MOVED:
            @pl.when(moves(slot, block))
            def _():
                stage[wave, block, slot] = inbox[wave][picked(slot, block)]
                cross_copy(wave, slot, block).start()

        for slot in (2, 3, 0, 1):
            @pl.when(jnp.logical_not(crosses(slot)))
            def _():
                feat[slot, mine, wave * WAVE : (wave + 1) * WAVE] = inbox[wave][
                    by_place(loaders, *SLOTS[slot])
                ]
                spread(wave, slot, 0)

    def spread_moved(kind):
        for slot, block in MOVED:
            @pl.when(moves(slot, block))
            def _():
                cross_copy(kind, slot, block).wait_recv()
                spread(kind, slot, block)

    def make_masks():
        for step in range(1, LOADERS):
            i_copy(step).wait_recv()
        for tile in range(2):
            loader = by_place(loaders, 0, tile)
            place = by_place(places, 0, tile)
            line = ids[loader, pl.ds(place, 1), :].astype(F32)
            across = jnp.broadcast_to(line, (PATCH, PATCH))
            mask[tile] = (across == across.T).astype(F32)

    def project_back(unit):
        half = unit // HALF
        tiles = pl.ds(2 * lax.rem(unit, HALF), 2)
        lines = pl.ds(pl.multiple_of(half * QKV, HEAD), QKV)
        product = dot(cot[tiles].reshape(2 * PATCH, BOTH), w_out[lines, :], NT).astype(BF)
        part[half, tiles] = product.reshape(2, PATCH, QKV)

    def project(unit):
        group = unit // HALF
        tiles = pl.ds(2 * lax.rem(unit, HALF), 2)
        columns = pl.ds(pl.multiple_of((group - 2) * QKV, HEAD), QKV)
        product = dot(feat[tiles].reshape(2 * PATCH, BOTH), w_qkv[:, columns], NN).astype(BF)
        part[group, tiles] = product.reshape(2, PATCH, QKV)

    def run(function, start, stop):
        def step(unit, carry):
            function(unit)
            return carry

        lax.fori_loop(start, stop, step, 0)

    def b_copy(group, which):
        return remote(
            part.at[group, 2 + which], chain.at[group, which],
            b_send.at[group, which], b_recv.at[group, which], (left, right)[which],
        )

    def c_copy(head, which):
        return remote(
            found.at[head, which], found.at[head, 2 + which],
            c_send.at[head, which], c_recv.at[head, which], (right, left)[which],
        )

    def b_first(group):
        for which in range(2):
            b_copy(group, which).start()

    def b_total(group, which):
        b_copy(group, which).wait_recv()
        return part[group, which].astype(F32) + chain[group, which].astype(F32)

    def c_first(head):
        for which in range(2):
            c_copy(head, which).start()

    def attend_head(head):
        columns = pl.ds(pl.multiple_of(lax.rem(head, 3) * HEAD, HEAD), HEAD)
        totals = [b_total(head + 2, tile) for tile in range(2)]
        for tile in range(2):
            found[head, tile] = attend(
                totals[tile], part[head // 3, tile, :, columns], mask[tile]
            )
        c_first(head)

    spread_moved(WAVES)
    w_spread(0)
    for wave in range(WAVES):
        take_wave(wave)
        if wave == 0:
            w_spread(1)
        else:
            spread_moved(wave - 1)
    w_share(0)
    spread_moved(WAVES - 1)
    w_share(1)
    make_masks()
    for slot in range(HELD):
        @pl.when(jnp.logical_not(crosses(slot)))
        def _():
            cot_load(slot).wait()

    for slot, block in MOVED:
        @pl.when(moves(slot, block))
        def _():
            gather(WAVES, slot, block)

    loads[1].wait()
    w_wait(0)
    run(project_back, 0, BACKS)
    for group in range(2):
        b_first(group)
    for wave in range(WAVES):
        for slot in range(HELD):
            for block in range(2):
                gather(wave, slot, block)
    loads[2].wait()
    w_wait(1)
    run(project, BACKS, BACKS + HALF)
    b_first(2)
    for group in range(2):
        for tile in range(2):
            part[group, tile] = b_total(group, tile).astype(BF)

    feat_acc[...] = jnp.zeros_like(feat_acc)

    def core_copy(chunk):
        return remote(
            grads.at[chunk, :, :, 1 - core], core_in.at[chunk],
            core_send.at[chunk], core_recv.at[chunk], core_peer,
        )

    def y_copy(chunk, step):
        return remote(
            core_sum.at[chunk, :, pl.ds(2 * lax.rem(row + step, 4), 2)], y_in.at[chunk, step - 1],
            y_send.at[chunk, step - 1], y_recv.at[chunk, step - 1], row_peer(step),
        )

    def high_peers(which):
        return (high_peer, (dp, opposite(1), my), (turned, opposite(1), my))[which]

    def high_part(held, which):
        return (held.at[0, 1 - high], held.at[1, high], held.at[1, 1 - high])[which]

    def z_copy(chunk, which):
        return remote(
            high_part(y_sum.at[chunk], which), z_in.at[chunk, which],
            z_send.at[chunk, which], z_recv.at[chunk, which], high_peers(which),
        )

    def stage_core(chunk):
        core_copy(chunk).wait_recv()
        core_sum[chunk] = (
            grads[chunk, :, :, core].astype(F32) + core_in[chunk].astype(F32)
        ).astype(BF)
        for step in (2, 1, 3):
            y_copy(chunk, step).start()

    def stage_row(chunk):
        total = core_sum[chunk, :, pl.ds(2 * row, 2)].astype(F32)
        for step in (1, 3, 2):
            y_copy(chunk, step).wait_recv()
            total = total + y_in[chunk, step - 1].astype(F32)
        y_sum[chunk] = total.astype(BF)
        for which in range(3):
            z_copy(chunk, which).start()

    def stage_high(chunk):
        total = y_sum[chunk, 0, high].astype(F32)
        for which in (1, 2, 0):
            z_copy(chunk, which).wait_recv()
            total = total + z_in[chunk, which].astype(F32)
        return total * (1.0 / 16.0)

    def store_qkv(chunk):
        columns = pl.ds(pl.multiple_of(chunk * QKV, HEAD), QKV)
        out_qkv[0, :, columns] = stage_high(chunk)

    def back_pair(head, pair):
        tiles = pl.ds(2 * pair, 2)
        columns = pl.ds(pl.multiple_of(head * QKV, HEAD), QKV)
        back = dot(found[head, tiles, :, HEAD:].reshape(2 * PATCH, QKV), w_qkv[:, columns], NT)
        feat_acc[tiles] += back.reshape(2, PATCH, BOTH)

    def d_copy(pair, step):
        lines = pl.ds(pl.multiple_of(lax.rem(my + step, 4) * QUARTER, QUARTER), QUARTER)
        tiles = pl.ds(2 * pair, 2)
        return remote(
            feat_bf.at[tiles, lines], feat_in.at[step - 1, tiles],
            d_send.at[pair, step - 1], d_recv.at[pair, step - 1], x_peer(step),
        )

    def d_start(pair):
        tiles = pl.ds(2 * pair, 2)
        feat_bf[tiles] = feat_acc[tiles].astype(BF)
        for step in (2, 1, 3):
            d_copy(pair, step).start()

    def d_finish(pair):
        for step in (1, 3, 2):
            d_copy(pair, step).wait_recv()
        for slot in (2 * pair, 2 * pair + 1):
            total = feat_acc[slot, mine, :]
            for step in (1, 3, 2):
                total = total + feat_in[step - 1, slot].astype(F32)
            total = total.astype(BF)
            for block in (1, 0):
                @pl.when(moves(slot, block))
                def _():
                    back_out[slot, block] = total[:, block * WIDE : (block + 1) * WIDE]
                    return_copy(slot, block).start()

            @pl.when(jnp.logical_not(crosses(slot)))
            def _():
                out_feat[tile_of(slot)] = total[:, :WIDE]

    def half_core_copy(half):
        return remote(
            half_grad.at[half, :, :, 1 - core], half_in.at[half],
            half_core_send.at[half], half_core_recv.at[half], core_peer,
        )

    def half_row_copy(step):
        to = lax.rem(row + step, 4)
        return remote(
            half_sum.at[to // 2, :, pl.ds(2 * lax.rem(to, 2), 2)], half_y.at[step - 1],
            half_row_send.at[step - 1], half_row_recv.at[step - 1], row_peer(step),
        )

    def half_high_copy(which):
        return remote(
            high_part(half_ysum, which), half_z.at[which],
            half_high_send.at[which], half_high_recv.at[which], high_peers(which),
        )

    def half_begin(half):
        lines = slice(half * HALF_ROWS, (half + 1) * HALF_ROWS)
        for block in range(2):
            half_grad[half, block] = grad_wide[
                lines, block * WIDE : (block + 1) * WIDE
            ].reshape(4, 2, 48, WIDE)
        half_core_copy(half).start()

    def half_stage_core(half):
        half_core_copy(half).wait_recv()
        half_sum[half] = (
            half_grad[half, :, :, core].astype(F32) + half_in[half].astype(F32)
        ).astype(BF)
        for step in (2, 1, 3):
            @pl.when(lax.rem(row + step, 4) // 2 == half)
            def _():
                half_row_copy(step).start()

    def half_stage_row(half):
        @pl.when(row // 2 == half)
        def _():
            total = half_sum[half, :, pl.ds(2 * lax.rem(row, 2), 2)].astype(F32)
            for step in (1, 3, 2):
                half_row_copy(step).wait_recv()
                total = total + half_y[step - 1].astype(F32)
            half_ysum[...] = total.astype(BF)
            for which in range(3):
                half_high_copy(which).start()

    def half_stage_high(half):
        @pl.when(row // 2 == half)
        def _():
            total = half_ysum[0, high].astype(F32)
            for which in (1, 2, 0):
                half_high_copy(which).wait_recv()
                total = total + half_z[which].astype(F32)
            out_out[0] = total * (1.0 / 16.0)

    def weight_piece(head, at):
        grad = found[head, :, :, HEAD:].reshape(HELD * PATCH, QKV)
        lines = pl.ds(pl.multiple_of(at * HALF_ROWS, HALF_ROWS), HALF_ROWS)
        piece = dot(feat_t[lines, :], grad, NN).astype(BF)
        grads[head, at // 2, pl.ds(4 * lax.rem(at, 2), 4)] = piece.reshape(4, 2, 48, QKV)

    def weights(head):
        lines = pl.ds(pl.multiple_of(head * HEAD, HEAD), HEAD)
        grad_wide[lines, :] = dot(
            found[head, :, :, :HEAD].reshape(HELD * PATCH, HEAD),
            cot[...].reshape(HELD * PATCH, BOTH),
            TN,
        ).astype(BF)
        for half in range(2):
            @pl.when(head == 3 * half + 2)
            def _():
                half_begin(half)

        run(lambda at: weight_piece(head, at), 0, 4)
        core_copy(head).start()

    def near_rows(head):
        back_pair(head, 0)

        @pl.when(head == HEADS_HERE - 1)
        def _():
            d_start(0)

    def far_rows(head):
        for which in range(2):
            c_copy(head, which).wait_recv()
        back_pair(head, 1)

        @pl.when(head == HEADS_HERE - 1)
        def _():
            d_start(1)

    def when(least, head, function):
        @pl.when((head >= least) & (head < HEADS_HERE))
        def _():
            function(head)

    def head_step(now):
        when(1, now, lambda head: b_first(head + 2))
        when(1, now + 1, lambda head: run(project, BACKS + HALF * head, BACKS + HALF * head + HALF))
        when(0, now - 1, attend_head)

        @pl.when(now < 2)
        def _():
            for slot in range(2):
                columns = pl.ds(pl.multiple_of((2 * now + slot) * PATCH, PATCH), PATCH)
                feat_t[:, columns] = feat[2 * now + slot].T

        @pl.when(now >= 3)
        def _():
            stage_core(now - 3)

        @pl.when(now >= 5)
        def _():
            stage_row(now - 5)

        @pl.when(now >= 6)
        def _():
            store_qkv(now - 6)

        for later, stage_half in ((5, half_stage_core), (7, half_stage_row)):
            @pl.when(now == later)
            def _():
                stage_half(0)

        when(0, now - 1, near_rows)
        when(0, now - 2, far_rows)
        when(0, now - 2, weights)

    run(head_step, 0, HEADS_HERE + 2)

    half_stage_core(1)
    stage_core(5)
    d_finish(0)
    stage_row(3)
    store_qkv(2)
    d_finish(1)
    stage_row(4)
    half_stage_row(1)
    store_qkv(3)
    half_stage_high(0)
    stage_row(5)
    store_qkv(4)
    half_stage_high(1)
    store_qkv(5)
    for slot, block in MOVED:
        @pl.when(moves(slot, block))
        def _():
            return_copy(slot, block).wait_recv()
            out_feat[sent_tile(slot, block)] = back_in[slot, block]

    for step in range(1, LOADERS):
        for wave in range(WAVES):
            a_copy(wave, step).wait_send()
        i_copy(step).wait_send()
    for step in range(1, 4):
        for pair in range(2):
            d_copy(pair, step).wait_send()
        half_row_copy(step).wait_send()
    for half in range(2):
        half_core_copy(half).wait_send()
    for which in range(3):
        half_high_copy(which).wait_send()
    for slot, block in MOVED:
        @pl.when(moves(slot, block))
        def _():
            for kind in range(WAVES + 1):
                cross_copy(kind, slot, block).wait_send()
            return_copy(slot, block).wait_send()
            for step in range(1, 4):
                spread_copy(WAVES, slot, block, step).wait_send()

        for step in range(1, 4):
            for wave in range(WAVES):
                spread_copy(wave, slot, block, step).wait_send()
    for kind in range(2):
        w_far_copy(kind).wait_send()
        for step in range(4):
            w_core_copy(kind, step).wait_send()
        for step in range(1, 4):
            w_row_copy(kind, step).wait_send()

    def drain(chunk, carry):
        core_copy(chunk).wait_send()
        for which in range(3):
            z_copy(chunk, which).wait_send()
        for step in range(1, 4):
            y_copy(chunk, step).wait_send()
        return carry

    lax.fori_loop(0, CHUNKS, drain, 0)

    def drain_group(group):
        for which in range(2):
            b_copy(group, which).wait_send()

    def drain_head(head):
        for which in range(2):
            c_copy(head, which).wait_send()

    run(drain_group, 0, GROUPS)
    run(drain_head, 0, HEADS_HERE)


def shards(features, segment_ids, owners, w_qkv, w_out, cotangent):
    vmem = pl.BlockSpec(memory_space=pltpu.VMEM)
    hbm = pl.BlockSpec(memory_space=pl.ANY)
    smem = pl.BlockSpec(memory_space=pltpu.SMEM)
    dma = pltpu.SemaphoreType.DMA
    units = (HEADS_HERE, TILES, PATCH, UNIT)
    sums = (GROUPS, TILES, PATCH, QKV)
    return pl.pallas_call(
        branch,
        out_shape=(
            jax.ShapeDtypeStruct((TILES, 32, WIDE), BF),
            jax.ShapeDtypeStruct((1, 48, HEADS_HERE * QKV), F32),
            jax.ShapeDtypeStruct((1, 48, WIDE), F32),
        ),
        in_specs=[smem, hbm, vmem, hbm, hbm, hbm],
        out_specs=(vmem,) * 3,
        scratch_shapes=[
            pltpu.VMEM((TILES, QUARTER, WIDE), BF),
            pltpu.VMEM((BOTH, HEADS_HERE * QKV), BF),
            pltpu.VMEM((HEADS_HERE * HEAD, BOTH), BF),
            dma((3 + HELD,)),
            pltpu.VMEM((HELD, PATCH, BOTH), BF),
            pltpu.VMEM((HELD, PATCH, BOTH), BF),
            pltpu.VMEM((BOTH, HELD * PATCH), BF),
            pltpu.VMEM((GROUPS, HELD, PATCH, QKV), BF),
            pltpu.VMEM((GROUPS, 2, PATCH, QKV), BF),
            pltpu.VMEM((HEADS_HERE, HELD, PATCH, UNIT), BF),
            pltpu.VMEM((CHUNKS, 2, 8, 2, 48, QKV), BF),
            pltpu.VMEM((CHUNKS, 2, 8, 48, QKV), BF),
            pltpu.VMEM((CHUNKS, 2, 8, 48, QKV), BF),
            pltpu.VMEM((CHUNKS, 3, 2, 2, 48, QKV), BF),
            pltpu.VMEM((CHUNKS, 2, 2, 48, QKV), BF),
            pltpu.VMEM((CHUNKS, 3, 48, QKV), BF),
            pltpu.VMEM((2, 2, 4, 2, 48, WIDE), BF),
            pltpu.VMEM((2, 2, 4, 48, WIDE), BF),
            pltpu.VMEM((2, 2, 4, 48, WIDE), BF),
            pltpu.VMEM((3, 2, 2, 48, WIDE), BF),
            pltpu.VMEM((2, 2, 48, WIDE), BF),
            pltpu.VMEM((3, 48, WIDE), BF),
            pltpu.VMEM((WIDE, BOTH), BF),
            pltpu.VMEM((HELD, PATCH, BOTH), F32),
            pltpu.VMEM((HELD, PATCH, BOTH), BF),
            pltpu.VMEM((3, HELD, QUARTER, BOTH), BF),
            pltpu.VMEM((WAVES, LOADERS, QUARTER, WAVE), BF),
            pltpu.VMEM((LOADERS, QUARTER, WAVE), BF),
            pltpu.VMEM((LOADERS, QUARTER, WAVE), BF),
            pltpu.VMEM((LOADERS, TILES, PATCH), jnp.int32),
            pltpu.VMEM((2, PATCH, PATCH), F32),
            dma((2,)), dma((2,)), dma((2, 3)), dma((2, 3)), dma((2, 4)), dma((2, 4)),
            pltpu.VMEM((WAVES, 2, HELD, QUARTER, WAVE), BF),
            pltpu.VMEM((HELD, 2, QUARTER, WIDE), BF),
            pltpu.VMEM((HELD, 2, QUARTER, WIDE), BF),
            dma((WAVES + 2, HELD, 2)), dma((WAVES + 2, HELD, 2)),
            dma((WAVES + 1, HELD, 2, 3)), dma((WAVES + 1, HELD, 2, 3)),
            dma((WAVES, LOADERS - 1)), dma((WAVES, LOADERS - 1)),
            dma((LOADERS - 1,)), dma((LOADERS - 1,)),
            dma((GROUPS, 2)), dma((GROUPS, 2)),
            dma((HEADS_HERE, 2)), dma((HEADS_HERE, 2)),
            dma((2,)), dma((2,)), dma((3,)), dma((3,)), dma((3,)), dma((3,)),
            dma((CHUNKS,)), dma((CHUNKS,)),
            dma((CHUNKS, 3)), dma((CHUNKS, 3)),
            dma((CHUNKS, 3)), dma((CHUNKS, 3)),
            dma((2, 3)), dma((2, 3)),
        ],
        compiler_params=pltpu.CompilerParams(
            collective_id=0, has_side_effects=True, vmem_limit_bytes=60 * 1024 * 1024
        ),
        cost_estimate=pl.CostEstimate(
            flops=14_000_000_000, bytes_accessed=12_000_000, transcendentals=400_000
        ),
    )(owners, features, segment_ids, cotangent, w_qkv, w_out)


def solution(mesh):
    return jax.shard_map(
        shards,
        mesh=mesh,
        in_specs=(
            P("dp", None, "mx"),
            P("dp", None),
            P(),
            P("mx", "my"),
            P("my", "mx"),
            P("dp", None, "mx"),
        ),
        out_specs=(P("dp", "my", "mx"), P("mx", "dp", "my"), P("my", "dp", "mx")),
        check_vma=False,
    )
```

time: 199 us -> 191 us (0.960)
  the two profiles are of different devices: /device:TPU:1 before, /device:TPU:31 now
where the time goes in v5:
time: 191 us
  Pallas kernels  185 us (97%)
  local copies, waits for them, and re-layouts  5.63 us (3%)
    pallas_call x1, Pallas kernels, shards(): pl.pallas_call(branch, out_shape=(jax.ShapeDtypeStruct((TILES, 32, WIDE),...  185 us
    unnamed x6, local copies, waits for them, and re-layouts  5.63 us

profile of v5, /device:TPU:31, one launch (start us, length us, event | category | flops | bytes accessed | tf_op | source)
XLA Modules:
  0.0 191.2 jit_solution(1260909588744984098)
XLA Ops:
  0.6 1.4 copy.9.owners
  2.0 184.9 %shard_map.85 = (bf16[8,32,768]{2,1,0:T(8,128)(2,1)}, f32[1,48,2304]{2,1,0:T(8,128)}, f32[1,48,768]{2,1,0:T(8,128)}) custom-call(s32[16,8]{1,0:T(8,128)} %copy.9.owners, bf16[8,128,768]{2,1,0:T(8,128)(2,1)} %features.1, s32[8,128]{1,0:T(8,128)} %given_ids.1, bf16[8,128,768]{2,1,0:T(8,128)(2,1)} %cot_given.1, bf16[768,2304]{1,0:T(8,128)(2,1)} %w_qkv_given.1, ...), custom_call_target="tpu_custom_call" | custom-call | flops 14000000000 | bytes 12000000 | tf_op jit(solution)/shard_map/pallas_call | solution.py:789
  186.9 0.0 copy-start
  186.9 1.8 copy.13
  188.7 1.8 copy.14
  190.5 0.0 copy-done
  190.5 0.7 copy.15
Async XLA Ops:
  186.9 3.6 %copy-start = (f32[1,48,768]{2,1,0:T(8,128)S(1)}, f32[1,48,768]{2,1,0:T(8,128)}, u32[]{:S(2)}) copy-start(f32[1,48,768]{2,1,0:T(8,128)} %get-tuple-element.8) | copy-start | bytes 442372

commit v6 on v5

--- a/solution.py
+++ b/solution.py
@@ -637,6 +637,8 @@
         grads[head, at // 2, pl.ds(4 * lax.rem(at, 2), 4)] = piece.reshape(4, 2, 48, QKV)
 
     def weights(head):
+        run(lambda at: weight_piece(head, at), 0, 4)
+        core_copy(head).start()
         lines = pl.ds(pl.multiple_of(head * HEAD, HEAD), HEAD)
         grad_wide[lines, :] = dot(
             found[head, :, :, :HEAD].reshape(HELD * PATCH, HEAD),
@@ -648,8 +650,6 @@
             def _():
                 half_begin(half)
 
-        run(lambda at: weight_piece(head, at), 0, 4)
-        core_copy(head).start()
 
     def near_rows(head):
         back_pair(head, 0)
@@ -675,6 +675,10 @@
     def head_step(now):
         when(1, now, lambda head: b_first(head + 2))
         when(1, now + 1, lambda head: run(project, BACKS + HALF * head, BACKS + HALF * head + HALF))
+        @pl.when(now >= 3)
+        def _():
+            stage_core(now - 3)
+
         when(0, now - 1, attend_head)
 
         @pl.when(now < 2)
@@ -682,10 +686,6 @@
             for slot in range(2):
                 columns = pl.ds(pl.multiple_of((2 * now + slot) * PATCH, PATCH), PATCH)
                 feat_t[:, columns] = feat[2 * now + slot].T
-
-        @pl.when(now >= 3)
-        def _():
-            stage_core(now - 3)
 
         @pl.when(now >= 5)
         def _():

time: 191 us -> 191 us (level)
  the two profiles are of different devices: /device:TPU:31 before, /device:TPU:1 now
where the time goes in v6:
time: 191 us; the launch traced here: 188 us
  Pallas kernels  181 us (95%)
  local copies, waits for them, and re-layouts  5.63 us (3%)
    pallas_call x1, Pallas kernels, shards(): pl.pallas_call(branch, out_shape=(jax.ShapeDtypeStruct((TILES, 32, WIDE),...  181 us
    unnamed x6, local copies, waits for them, and re-layouts  5.63 us

profile of v6, /device:TPU:1, one launch (start us, length us, event | category | flops | bytes accessed | tf_op | source)
XLA Modules:
  0.0 187.7 jit_solution(978713229517839253)
XLA Ops:
  0.6 1.4 copy.9.owners
  2.0 181.4 %shard_map.85 = (bf16[8,32,768]{2,1,0:T(8,128)(2,1)}, f32[1,48,2304]{2,1,0:T(8,128)}, f32[1,48,768]{2,1,0:T(8,128)}) custom-call(s32[16,8]{1,0:T(8,128)} %copy.9.owners, bf16[8,128,768]{2,1,0:T(8,128)(2,1)} %features.1, s32[8,128]{1,0:T(8,128)} %given_ids.1, bf16[8,128,768]{2,1,0:T(8,128)(2,1)} %cot_given.1, bf16[768,2304]{1,0:T(8,128)(2,1)} %w_qkv_given.1, ...), custom_call_target="tpu_custom_call" | custom-call | flops 14000000000 | bytes 12000000 | tf_op jit(solution)/shard_map/pallas_call | solution.py:789
  183.4 0.0 copy-start
  183.4 1.8 copy.13
  185.2 1.8 copy.14
  187.0 0.0 copy-done
  187.0 0.7 copy.15
Async XLA Ops:
  183.4 3.6 %copy-start = (f32[1,48,768]{2,1,0:T(8,128)S(1)}, f32[1,48,768]{2,1,0:T(8,128)}, u32[]{:S(2)}) copy-start(f32[1,48,768]{2,1,0:T(8,128)} %get-tuple-element.8) | copy-start | bytes 442372
